TPU v7x, 32 devices: a whole 2x2x4 slice. The times are simulated.
32 devices in a mesh: sx: 2 (over y), sy: 4 (over z), vel: 4 (over x, core).
Axes of the slice: x: 2, y: 2, z: 4, core: 2. Of those that a mesh axis runs over, the one named last changes fastest.
Arguments:
- distribution: float32 [32, 128, 13824], P('sx', 'sy', 'vel'), as said below
- cell_kind: int32 [32, 128], P('sx', 'sy'), may hold values from 0 to 2, as said below
- local_knudsen: float32 [32, 128], P('sx', 'sy'), may hold values from 0.3 to 30
Outputs:
- evolved: float32 [32, 128, 13824], P('sx', 'sy', 'vel')
Inputs may be any that keep to these rules, and one draw needn't show every extreme that they name: `cell_kind`: 0 marks a gas cell, 1 a wall cell, 2 an inflow cell. `distribution`: every entry is positive.
All inputs are finite; a program needn't handle non-finite values.
Results may differ from a plain program's by a relative error of at most 0.0003.
Values sent between devices are 32-bit elements; how exact they have to be, the bound alone decides.
A program may use at most 128 MiB of HBM per device.

v0:
```python
import math

import jax
import jax.numpy as jnp
from jax import lax
from jax.sharding import PartitionSpec as P

NVX = 24
STEPS = 2


VEL_LIMIT = 4.8
CLOCK_ADVANCE = 0.09
VISCOUS_RATIO = 2.0 / 3.0
WALL_TEMP = 1.0
INFLOW_DENSITY = 12.0
INFLOW_SPEED = 0.5
INFLOW_TEMP = 1.0


def extended(shard, sides, width):
    for axis, dim in sides:
        devices, length = (lax.axis_size(axis), shard.shape[dim])
        up = [(i, (i + 1) % devices) for i in range(devices)]
        down = [(j, i) for i, j in up]
        last = lax.slice_in_dim(shard, length - width, length, axis=dim)
        initial = lax.slice_in_dim(shard, 0, width, axis=dim)
        before = lax.ppermute(last, axis, up)
        after = lax.ppermute(initial, axis, down)
        shard = jnp.concatenate([before, shard, after], axis=dim)
    return shard


def widen_last_index(value):
    return value[..., None]


def line_value(points):
    spacing = 2.0 * VEL_LIMIT / NVX
    return (
        ((points // 2).astype(jnp.float32) + 0.5)
        * spacing
        * (2 * (points % 2) - 1).astype(jnp.float32)
    )


def conserved_integrals(quadrature_totals):
    molecule_crowding = quadrature_totals[0]
    mean_motion_x = quadrature_totals[1] / molecule_crowding
    mean_motion_y = quadrature_totals[2] / molecule_crowding
    mean_motion_z = quadrature_totals[3] / molecule_crowding
    molecular_agitation = (
        quadrature_totals[4] / molecule_crowding
        - (
            mean_motion_x * mean_motion_x
            + mean_motion_y * mean_motion_y
            + mean_motion_z * mean_motion_z
        )
    ) / 3.0
    return (molecule_crowding, mean_motion_x, mean_motion_y, mean_motion_z, molecular_agitation)


def relax(present_state, macro_integrals, local_knudsen, cell_kind, speed_x, speed_y, speed_z):
    (
        molecule_crowding,
        mean_motion_x,
        mean_motion_y,
        mean_motion_z,
        molecular_agitation,
        conduction_x,
        conduction_y,
        conduction_z,
    ) = macro_integrals
    relative_motion_component = speed_x - widen_last_index(mean_motion_x)
    drift_y = speed_y - widen_last_index(mean_motion_y)
    drift_z = speed_z - widen_last_index(mean_motion_z)
    relative_motion_norm = (
        relative_motion_component * relative_motion_component
        + drift_y * drift_y
        + drift_z * drift_z
    )
    maxwell_profile = widen_last_index(
        molecule_crowding / (2.0 * math.pi * molecular_agitation) ** 1.5
    ) * jnp.exp(-relative_motion_norm / widen_last_index(2.0 * molecular_agitation))
    thermal_dot_offset = (
        relative_motion_component * widen_last_index(conduction_x)
        + drift_y * widen_last_index(conduction_y)
        + drift_z * widen_last_index(conduction_z)
    )
    leading_coefficient = (
        (1.0 - VISCOUS_RATIO)
        * thermal_dot_offset
        / widen_last_index(5.0 * molecule_crowding * molecular_agitation * molecular_agitation)
        * (relative_motion_norm / widen_last_index(molecular_agitation) - 5.0)
    )
    shakhov_closure_model = maxwell_profile * (1.0 + leading_coefficient)
    remaining_indicator = jnp.exp(
        -CLOCK_ADVANCE * molecule_crowding * jnp.sqrt(molecular_agitation) / local_knudsen
    )
    medium_cells = shakhov_closure_model + (
        present_state - shakhov_closure_model
    ) * widen_last_index(remaining_indicator)
    speed_sq = speed_x * speed_x + speed_y * speed_y + speed_z * speed_z
    wall = widen_last_index(molecule_crowding / (2.0 * math.pi * WALL_TEMP) ** 1.5) * jnp.exp(
        -speed_sq / (2.0 * WALL_TEMP)
    )
    shifted = speed_x - INFLOW_SPEED
    inflow = (
        INFLOW_DENSITY
        / (2.0 * math.pi * INFLOW_TEMP) ** 1.5
        * jnp.exp(
            -(shifted * shifted + speed_y * speed_y + speed_z * speed_z) / (2.0 * INFLOW_TEMP)
        )
    )
    return jnp.where(
        widen_last_index(cell_kind == 1),
        wall,
        jnp.where(widen_last_index(cell_kind == 2), inflow, medium_cells),
    )


def minmod(left, right):
    return 0.5 * (jnp.sign(left) + jnp.sign(right)) * jnp.minimum(jnp.abs(left), jnp.abs(right))


def sweep_strip(strip, speed, axis):
    length = strip.shape[axis]
    diff = lax.slice_in_dim(strip, 1, length, axis=axis) - lax.slice_in_dim(
        strip, 0, length - 1, axis=axis
    )
    slope = minmod(
        lax.slice_in_dim(diff, 0, length - 2, axis=axis),
        lax.slice_in_dim(diff, 1, length - 1, axis=axis),
    )
    cells = lax.slice_in_dim(strip, 1, length - 1, axis=axis)
    forward = jnp.maximum(speed, 0.0)
    backward = jnp.minimum(speed, 0.0)
    right = forward * (
        lax.slice_in_dim(cells, 0, length - 3, axis=axis)
        + 0.5 * lax.slice_in_dim(slope, 0, length - 3, axis=axis)
    ) + backward * (
        lax.slice_in_dim(cells, 1, length - 2, axis=axis)
        - 0.5 * lax.slice_in_dim(slope, 1, length - 2, axis=axis)
    )
    return lax.slice_in_dim(right, 1, length - 3, axis=axis) - lax.slice_in_dim(
        right, 0, length - 4, axis=axis
    )


def transport(strip_x, strip_y, speed_x, speed_y):
    centre = strip_x[2:-2]
    change = sweep_strip(strip_x, speed_x, 0) + sweep_strip(strip_y, speed_y, 1)
    return centre - CLOCK_ADVANCE * change


def face_strips(values):
    padded = extended(values, (("sx", 0), ("sy", 1)), 2)
    return (padded[:, 2:-2], padded[2:-2, :])


def moments(present_state, speed_x, speed_y, speed_z, weight):
    ones = jnp.ones_like(speed_x)
    speed_sq = speed_x * speed_x + speed_y * speed_y + speed_z * speed_z
    basis = jnp.stack([ones, speed_x, speed_y, speed_z, speed_sq]) * weight
    local = jnp.einsum("kv,xyv->kxy", basis, present_state, precision=lax.Precision.HIGHEST)
    quadrature_totals = lax.psum(local, "vel")
    molecule_crowding, mean_motion_x, mean_motion_y, mean_motion_z, molecular_agitation = (
        conserved_integrals(quadrature_totals)
    )
    relative_motion_component = speed_x - widen_last_index(mean_motion_x)
    drift_y = speed_y - widen_last_index(mean_motion_y)
    drift_z = speed_z - widen_last_index(mean_motion_z)
    relative_motion_norm = (
        relative_motion_component * relative_motion_component
        + drift_y * drift_y
        + drift_z * drift_z
    )
    weighted = relative_motion_norm * present_state
    partial_heat = jnp.stack(
        [
            jnp.sum(relative_motion_component * weighted, axis=-1),
            jnp.sum(drift_y * weighted, axis=-1),
            jnp.sum(drift_z * weighted, axis=-1),
        ]
    ) * (0.5 * weight)
    conduction_triple = lax.psum(partial_heat, "vel")
    conduction_x, conduction_y, conduction_z = (
        conduction_triple[0],
        conduction_triple[1],
        conduction_triple[2],
    )
    return (
        molecule_crowding,
        mean_motion_x,
        mean_motion_y,
        mean_motion_z,
        molecular_agitation,
        conduction_x,
        conduction_y,
        conduction_z,
    )


def body(distribution, cell_kind, local_knudsen):
    count = distribution.shape[2]
    index = lax.axis_index("vel") * count + jnp.arange(count, dtype=jnp.int32)
    spacing = 2.0 * VEL_LIMIT / NVX
    speed_x = line_value(index % NVX)
    speed_y = line_value(index // NVX % NVX)
    speed_z = line_value(index // (NVX * NVX))
    weight = spacing**3
    present_state = distribution
    for section_index in range(STEPS):
        macro_integrals = moments(present_state, speed_x, speed_y, speed_z, weight)
        relaxed = relax(
            present_state, macro_integrals, local_knudsen, cell_kind, speed_x, speed_y, speed_z
        )
        strip_x, strip_y = face_strips(relaxed)
        present_state = transport(strip_x, strip_y, speed_x, speed_y)
    return present_state


def solution(mesh):
    return jax.shard_map(
        body,
        mesh=mesh,
        in_specs=(P("sx", "sy", "vel"), P("sx", "sy"), P("sx", "sy")),
        out_specs=P("sx", "sy", "vel"),
        check_vma=False,
    )
```

profile of v0, /device:TPU:0, one launch (start us, length us, event | category | flops | bytes accessed | tf_op | source)
XLA Modules:
  0.0 390.0 jit_solution(2613393429879659171)
XLA Ops:
  0.0 0.4 fusion.115
  0.4 0.6 fusion.123
  1.0 0.1 fusion.75
  1.2 0.1 exponential_multiply_fusion
  1.3 0.1 stack.36
  1.4 0.0 copy-start.73
  1.4 0.0 copy-start.71
  1.5 16.4 %fusion.66 = f32[5,16,32]{2,0,1:T(8,128)S(1)} fusion(f32[16,32,3456]{2,1,0:T(8,128)} %param.3, f32[5,3456]{1,0:T(8,128)S(1)} %stack.36), kind=kOutput, calls=%fused_computation.130 | convolution fusion | flops 106185600 | bytes 7157248 | tf_op jit(solution)/shard_map/kv,xyv->kxy/dot_general | solution.py:165
  17.8 13.4 %psum.28 = f32[5,16,32]{2,0,1:T(8,128)S(1)} all-reduce(f32[5,16,32]{2,0,1:T(8,128)S(1)} %fusion.66), channel_id=1, replica_groups=mesh['sx'=2,'sy'=4,'vel'=4] {'vel'}, use_global_device_ids=true, to_apply=%region_0.1 | all-reduce | flops 2560 | bytes 20480 | tf_op jit(solution)/shard_map/psum | solution.py:166
  31.4 6.5 %fusion.22 = (f32[16,32]{1,0:T(8,128)S(1)}, f32[16,32]{1,0:T(8,128)S(1)}, f32[16,32]{1,0:T(8,128)S(1)}) fusion(f32[16,32]{1,0:T(8,128)S(1)} %get-tuple-element.18, f32[3456]{0:T(1024)S(1)} %get-tuple-element.52, f32[16,32,3456]{2,1,0:T(8,128)} %param.3, f32[16,32]{1,0:T(8,128)S(1)} %get-tuple-element.20, f32[3456]{0:T(1024)S(1)} %fusion.90, ...), kind=kLoop, calls=%fused_computation.76 | loop fusion | flops 26540544 | bytes 7131648 | tf_op jit(solution)/shard_map/reduce_sum | solution.py:181
  37.9 10.6 %psum.29 = f32[3,16,32]{2,1,0:T(8,128)S(1)} all-reduce(f32[3,16,32]{2,1,0:T(8,128)S(1)} %maximum_multiply_fusion), channel_id=1, replica_groups=mesh['sx'=2,'sy'=4,'vel'=4] {'vel'}, use_global_device_ids=true, to_apply=%region_4.5 | all-reduce | flops 1536 | bytes 12288 | tf_op jit(solution)/shard_map/psum | solution.py:186
  48.7 10.4 %select_select_fusion.1 = f32[16,32,3456]{2,1,0:T(8,128)S(1)} fusion(f32[16,32,3456]{2,1,0:T(8,128)} %param.3, f32[16,32]{1,0:T(8,128)S(1)} %get-tuple-element.44, f32[16,32]{1,0:T(8,128)S(1)} %get-tuple-element.51, f32[16,32]{1,0:T(8,128)S(1)} %get-tuple-element.43, f32[16,32]{1,0:T(8,128)S(1)} %get-tuple-element.41, f32[16,32]{1,0:T(8,128)S(1)} %get-tuple-element.42, ...), kind=kLoop, calls=%fused_computation.123 | loop fusion | flops 51314688 | bytes 14250496 | tf_op jit(solution)/shard_map/jit(_where)/select_n | solution.py:115
  59.2 0.1 fusion.139
  59.4 1.6 collective-permute-start.1
  61.0 0.5 collective-permute-start
  61.5 0.7 broadcast_minimum_fusion
  62.2 19.8 %collective-permute-done.1 = f32[2,32,3456]{2,1,0:T(8,128)S(1)} collective-permute-done((f32[2,32,3456]{2,1,0:T(8,128)S(1)}, f32[2,32,3456]{2,1,0:T(8,128)S(1)}, u32[]{:S(2)}, u32[]{:S(2)}) %collective-permute-start.1) | collective-permute-done | bytes 884768 | tf_op jit(solution)/shard_map/ppermute | solution.py:29
  82.0 17.7 %collective-permute-done = f32[2,32,3456]{2,1,0:T(8,128)S(1)} collective-permute-done((f32[2,32,3456]{2,1,0:T(8,128)S(1)}, f32[2,32,3456]{2,1,0:T(8,128)S(1)}, u32[]{:S(2)}, u32[]{:S(2)}) %collective-permute-start) | collective-permute-done | bytes 884768 | tf_op jit(solution)/shard_map/ppermute | solution.py:28
  99.7 0.4 pad_maximum_fusion.23
  100.1 0.1 copy.44
  100.1 3.7 collective-permute-start.3
  103.8 0.9 copy.42
  104.7 3.8 pad_maximum_fusion.14
  108.4 10.5 %slice_subtract_fusion.3 = f32[19,32,3456]{2,1,0:T(8,128)} fusion(f32[20,32,3456]{2,1,0:T(8,128)} %pad_maximum_fusion.14), kind=kLoop, calls=%fused_computation.53 | loop fusion | flops 2101248 | bytes 25214976 | tf_op jit(solution)/shard_map/sub | solution.py:128
  119.0 10.6 %minimum_multiply_fusion.3 = f32[18,32,3456]{2,1,0:T(8,128)} fusion(f32[19,32,3456]{2,1,0:T(8,128)} %slice_subtract_fusion.3), kind=kLoop, calls=%fused_computation.55 | loop fusion | flops 15925248 | bytes 23887872 | tf_op jit(solution)/shard_map/mul | solution.py:123
  129.6 8.6 %fusion.17 = f32[17,32,3456]{2,1,0:T(8,128)} fusion(f32[18,32,3456]{2,1,0:T(8,128)} %minimum_multiply_fusion.3, f32[2,32,3456]{2,1,0:T(8,128)S(1)} %collective-permute-done.1, f32[16,32,3456]{2,1,0:T(8,128)S(1)} %copy-done.1, f32[2,32,3456]{2,1,0:T(8,128)S(1)} %collective-permute-done, f32[3456]{0:T(1024)S(1)} %get-tuple-element.62, ...), kind=kLoop, calls=%fused_computation.68 | loop fusion | flops 16920576 | bytes 31435776 | tf_op jit(solution)/shard_map/add | solution.py:138
  138.2 0.3 copy.46
  138.5 1.4 copy.43
  139.9 0.8 copy-done.14
  140.7 5.1 %pad_maximum_fusion = f32[20,36,3456]{2,1,0:T(8,128)} fusion(f32[20,2,3456]{2,1,0:T(2,128)S(1)} %copy.46, f32[2,32,3456]{2,1,0:T(8,128)S(1)} %collective-permute-done.1, f32[16,32,3456]{2,1,0:T(8,128)S(1)} %copy-done.1, f32[2,32,3456]{2,1,0:T(8,128)S(1)} %collective-permute-done, f32[20,2,3456]{2,1,0:T(2,128)S(1)} %copy.43), kind=kLoop, calls=%fused_computation.18 | loop fusion | flops 9953280 | bytes 19906560 | tf_op jit(solution)/shard_map/concatenate | solution.py:30
  145.8 10.7 %slice_subtract_fusion.1 = f32[16,35,3456]{2,1,0:T(8,128)} fusion(f32[20,36,3456]{2,1,0:T(8,128)} %pad_maximum_fusion), kind=kLoop, calls=%fused_computation.44 | loop fusion | flops 1935360 | bytes 23224320 | tf_op jit(solution)/shard_map/sub | solution.py:128
  156.4 0.0 slice-start.6
  156.5 12.3 %minimum_multiply_fusion.1 = f32[16,34,3456]{2,1,0:T(8,128)S(1)} fusion(f32[16,35,3456]{2,1,0:T(8,128)} %slice_subtract_fusion.1), kind=kLoop, calls=%fused_computation.51 | loop fusion | flops 15040512 | bytes 22560768 | tf_op jit(solution)/shard_map/mul | solution.py:123
  168.8 0.0 slice-start.7
  169.0 15.8 %fusion.7 = f32[16,33,3456]{2,1,0:T(8,128)} fusion(f32[16,34,3456]{2,1,0:T(8,128)S(1)} %minimum_multiply_fusion.1, f32[20,2,3456]{2,1,0:T(2,128)S(1)} %copy.46, f32[2,32,3456]{2,1,0:T(8,128)S(1)} %copy-done.6, f32[16,32,3456]{2,1,0:T(8,128)S(1)} %bitcast.83, f32[2,32,3456]{2,1,0:T(8,128)S(1)} %copy-done.8, f32[20,2,3456]{2,1,0:T(2,128)} %copy-done.14, ...), kind=kLoop, calls=%fused_computation.37 | loop fusion | flops 23721984 | bytes 31878144 | tf_op jit(solution)/shard_map/add | solution.py:138
  185.0 15.0 %fusion.63 = f32[16,32,3456]{2,1,0:T(8,128)S(1)} fusion(f32[16,33,3456]{2,1,0:T(8,128)} %fusion.7, f32[17,32,3456]{2,1,0:T(8,128)} %fusion.17, f32[16,32]{1,0:T(8,128)S(1)} %copy-done.50, f32[16,32,3456]{2,1,0:T(8,128)S(1)} %bitcast.89, f32[16,32]{1,0:T(8,128)S(1)} %copy-done.54, f32[16,32]{1,0:T(8,128)S(1)} %copy-done.48, f32[16,32]{1,0:T(8,128)S(1)} %copy-done.58, ...), kind=kLoop, calls=%fused_computation.120 | loop fusion | flops 60162048 | bytes 42562048 | tf_op jit(solution)/shard_map/sub | solution.py:153
  200.0 3.0 copy-done.4
  203.0 14.3 %fusion.64 = f32[5,16,32]{2,0,1:T(8,128)S(1)} fusion(f32[16,32,3456]{2,1,0:T(8,128)S(1)} %fusion.63, f32[5,3456]{1,0:T(8,128)S(1)} %stack.36), kind=kOutput, calls=%fused_computation.128 | convolution fusion | flops 106185600 | bytes 7157248 | tf_op jit(solution)/shard_map/kv,xyv->kxy/dot_general | solution.py:165
  217.3 10.7 %psum.30 = f32[5,16,32]{2,1,0:T(8,128)S(1)} all-reduce(f32[5,16,32]{2,1,0:T(8,128)S(1)} %copy.48), channel_id=1, replica_groups=mesh['sx'=2,'sy'=4,'vel'=4] {'vel'}, use_global_device_ids=true, to_apply=%region_5.6 | all-reduce | flops 2560 | bytes 20480 | tf_op jit(solution)/shard_map/psum | solution.py:166
  228.1 6.5 %fusion.41 = (f32[16,32]{1,0:T(8,128)S(1)}, f32[16,32]{1,0:T(8,128)S(1)}, f32[16,32]{1,0:T(8,128)S(1)}) fusion(f32[16,32]{1,0:T(8,128)S(1)} %get-tuple-element.13, f32[3456]{0:T(1024)S(1)} %copy-done.17, f32[16,32,3456]{2,1,0:T(8,128)} %copy-done.4, f32[16,32]{1,0:T(8,128)S(1)} %get-tuple-element.15, f32[3456]{0:T(1024)S(1)} %copy-done.25, ...), kind=kLoop, calls=%fused_computation.95 | loop fusion | flops 26540544 | bytes 7131648 | tf_op jit(solution)/shard_map/reduce_sum | solution.py:181
  234.6 10.3 %psum.31 = f32[3,16,32]{2,1,0:T(8,128)S(1)} all-reduce(f32[3,16,32]{2,1,0:T(8,128)S(1)} %maximum_multiply_fusion.1), channel_id=1, replica_groups=mesh['sx'=2,'sy'=4,'vel'=4] {'vel'}, use_global_device_ids=true, to_apply=%region_9.10 | all-reduce | flops 1536 | bytes 12288 | tf_op jit(solution)/shard_map/psum | solution.py:186
  245.0 10.4 %select_select_fusion = f32[16,32,3456]{2,1,0:T(8,128)S(1)} fusion(f32[16,32,3456]{2,1,0:T(8,128)} %copy-done.4, f32[16,32]{1,0:T(8,128)S(1)} %get-tuple-element.35, f32[16,32]{1,0:T(8,128)S(1)} %get-tuple-element.46, f32[16,32]{1,0:T(8,128)S(1)} %get-tuple-element.34, f32[16,32]{1,0:T(8,128)S(1)} %get-tuple-element.38, f32[16,32]{1,0:T(8,128)S(1)} %get-tuple-element.39, ...), kind=kLoop, calls=%fused_computation.122 | loop fusion | flops 51314688 | bytes 14250496 | tf_op jit(solution)/shard_map/jit(_where)/select_n | solution.py:115
  255.4 0.1 fusion.138
  255.5 1.6 collective-permute-start.5
  257.1 0.5 collective-permute-start.4
  257.6 20.5 %collective-permute-done.5 = f32[2,32,3456]{2,1,0:T(8,128)S(1)} collective-permute-done((f32[2,32,3456]{2,1,0:T(8,128)S(1)}, f32[2,32,3456]{2,1,0:T(8,128)S(1)}, u32[]{:S(2)}, u32[]{:S(2)}) %collective-permute-start.5) | collective-permute-done | bytes 884768 | tf_op jit(solution)/shard_map/ppermute | solution.py:29
  278.2 17.7 %collective-permute-done.4 = f32[2,32,3456]{2,1,0:T(8,128)S(1)} collective-permute-done((f32[2,32,3456]{2,1,0:T(8,128)S(1)}, f32[2,32,3456]{2,1,0:T(8,128)S(1)}, u32[]{:S(2)}, u32[]{:S(2)}) %collective-permute-start.4) | collective-permute-done | bytes 884768 | tf_op jit(solution)/shard_map/ppermute | solution.py:28
  295.8 0.4 pad_maximum_fusion.21
  296.2 0.1 copy.51
  296.3 3.9 collective-permute-start.7
  300.1 0.9 copy.49
  301.0 4.0 %pad_maximum_fusion.15 = f32[20,32,3456]{2,1,0:T(8,128)} fusion(f32[2,32,3456]{2,1,0:T(8,128)S(1)} %collective-permute-done.5, f32[16,32,3456]{2,1,0:T(8,128)S(1)} %select_select_fusion, f32[2,32,3456]{2,1,0:T(8,128)S(1)} %collective-permute-done.4), kind=kLoop, calls=%fused_computation.49 | loop fusion | flops 4423680 | bytes 17694720 | tf_op jit(solution)/shard_map/concatenate | solution.py:30
  305.0 10.5 %slice_subtract_fusion.2 = f32[19,32,3456]{2,1,0:T(8,128)} fusion(f32[20,32,3456]{2,1,0:T(8,128)} %pad_maximum_fusion.15), kind=kLoop, calls=%fused_computation.52 | loop fusion | flops 2101248 | bytes 25214976 | tf_op jit(solution)/shard_map/sub | solution.py:128
  315.6 10.6 %minimum_multiply_fusion.2 = f32[18,32,3456]{2,1,0:T(8,128)} fusion(f32[19,32,3456]{2,1,0:T(8,128)} %slice_subtract_fusion.2), kind=kLoop, calls=%fused_computation.54 | loop fusion | flops 15925248 | bytes 23887872 | tf_op jit(solution)/shard_map/mul | solution.py:123
  326.2 8.6 %fusion.12 = f32[17,32,3456]{2,1,0:T(8,128)} fusion(f32[18,32,3456]{2,1,0:T(8,128)} %minimum_multiply_fusion.2, f32[2,32,3456]{2,1,0:T(8,128)S(1)} %collective-permute-done.5, f32[16,32,3456]{2,1,0:T(8,128)S(1)} %copy-done.3, f32[2,32,3456]{2,1,0:T(8,128)S(1)} %collective-permute-done.4, f32[3456]{0:T(1024)S(1)} %copy-done.40, f32[3456]{0:T(1024)S(1)} %copy-done.42), kind=kLoop, calls=%fused_computation.59 | loop fusion | flops 16920576 | bytes 31435776 | tf_op jit(solution)/shard_map/add | solution.py:138
  334.8 0.3 copy.53
  335.1 1.4 copy.50
  336.5 0.8 copy-done.13
  337.3 5.1 %pad_maximum_fusion.1 = f32[20,36,3456]{2,1,0:T(8,128)} fusion(f32[20,2,3456]{2,1,0:T(2,128)S(1)} %copy.53, f32[2,32,3456]{2,1,0:T(8,128)S(1)} %collective-permute-done.5, f32[16,32,3456]{2,1,0:T(8,128)S(1)} %copy-done.3, f32[2,32,3456]{2,1,0:T(8,128)S(1)} %collective-permute-done.4, f32[20,2,3456]{2,1,0:T(2,128)S(1)} %copy.50), kind=kLoop, calls=%fused_computation.19 | loop fusion | flops 9953280 | bytes 19906560 | tf_op jit(solution)/shard_map/concatenate | solution.py:30
  342.4 10.7 %slice_subtract_fusion = f32[16,35,3456]{2,1,0:T(8,128)} fusion(f32[20,36,3456]{2,1,0:T(8,128)} %pad_maximum_fusion.1), kind=kLoop, calls=%fused_computation.30 | loop fusion | flops 1935360 | bytes 23224320 | tf_op jit(solution)/shard_map/sub | solution.py:128
  353.1 12.3 %minimum_multiply_fusion = f32[16,34,3456]{2,1,0:T(8,128)S(1)} fusion(f32[16,35,3456]{2,1,0:T(8,128)} %slice_subtract_fusion), kind=kLoop, calls=%fused_computation.50 | loop fusion | flops 15040512 | bytes 22560768 | tf_op jit(solution)/shard_map/mul | solution.py:123
  365.4 0.0 slice-start.5
  365.5 7.2 %fusion.2 = f32[16,33,3456]{2,1,0:T(8,128)} fusion(f32[16,34,3456]{2,1,0:T(8,128)S(1)} %minimum_multiply_fusion, f32[20,2,3456]{2,1,0:T(2,128)S(1)} %copy.53, f32[2,32,3456]{2,1,0:T(8,128)S(1)} %copy-done.10, f32[16,32,3456]{2,1,0:T(8,128)S(1)} %bitcast.85, f32[2,32,3456]{2,1,0:T(8,128)S(1)} %copy-done.12, f32[20,2,3456]{2,1,0:T(2,128)} %copy-done.13, ...), kind=kLoop, calls=%fused_computation.23 | loop fusion | flops 23721984 | bytes 31878144 | tf_op jit(solution)/shard_map/add | solution.py:138
  372.8 16.7 %fusion.60 = f32[16,32,3456]{2,1,0:T(8,128)} fusion(f32[16,33,3456]{2,1,0:T(8,128)} %fusion.2, f32[17,32,3456]{2,1,0:T(8,128)} %fusion.12, f32[16,32]{1,0:T(8,128)S(1)} %get-tuple-element.35, f32[16,32,3456]{2,1,0:T(8,128)S(1)} %bitcast.87, f32[16,32]{1,0:T(8,128)S(1)} %get-tuple-element.46, f32[16,32]{1,0:T(8,128)S(1)} %get-tuple-element.34, ...), kind=kLoop, calls=%fused_computation.115 | loop fusion | flops 60162048 | bytes 42562048 | tf_op jit(solution)/shard_map/sub | solution.py:153
  (180 shorter events, 0.6 us)
Async XLA Ops:
  1.1 47.5 %copy-start.15 = (f32[3456]{0:T(1024)}, f32[3456]{0:T(1024)S(1)}, u32[]{:S(2)}) copy-start(f32[3456]{0:T(1024)S(1)} %get-tuple-element.52) | copy-start | bytes 41476
  1.1 47.5 %copy-start.19 = (f32[3456]{0:T(1024)}, f32[3456]{0:T(1024)S(1)}, u32[]{:S(2)}) copy-start(f32[3456]{0:T(1024)S(1)} %get-tuple-element.53) | copy-start | bytes 41476
  1.2 47.5 %copy-start.23 = (f32[3456]{0:T(1024)}, f32[3456]{0:T(1024)S(1)}, u32[]{:S(2)}) copy-start(f32[3456]{0:T(1024)S(1)} %fusion.90) | copy-start | bytes 41476
  1.3 47.4 %copy-start.27 = (f32[3456]{0:T(1024)}, f32[3456]{0:T(1024)S(1)}, u32[]{:S(2)}) copy-start(f32[3456]{0:T(1024)S(1)} %get-tuple-element.54) | copy-start | bytes 41476
  1.3 47.4 %copy-start.31 = (f32[3456]{0:T(1024)}, f32[3456]{0:T(1024)S(1)}, u32[]{:S(2)}) copy-start(f32[3456]{0:T(1024)S(1)} %get-tuple-element.55) | copy-start | bytes 41476
  1.4 47.0 %copy-start.73 = (s32[16,32]{1,0:T(8,128)S(1)}, s32[16,32]{1,0:T(8,128)}, u32[]{:S(2)}) copy-start(s32[16,32]{1,0:T(8,128)} %param.4) | copy-start | bytes 6148
  1.4 47.1 %copy-start.71 = (f32[16,32]{1,0:T(8,128)S(1)}, f32[16,32]{1,0:T(8,128)}, u32[]{:S(2)}) copy-start(f32[16,32]{1,0:T(8,128)} %param.5) | copy-start | bytes 6148
  31.3 27.8 %copy-start.43 = (f32[16,32]{1,0:T(8,128)}, f32[16,32]{1,0:T(8,128)S(1)}, u32[]{:S(2)}) copy-start(f32[16,32]{1,0:T(8,128)S(1)} %get-tuple-element.19) | copy-start | bytes 6148
  31.3 27.8 %copy-start.45 = (f32[16,32]{1,0:T(8,128)}, f32[16,32]{1,0:T(8,128)S(1)}, u32[]{:S(2)}) copy-start(f32[16,32]{1,0:T(8,128)S(1)} %get-tuple-element.20) | copy-start | bytes 6148
  31.4 27.8 %copy-start.61 = (f32[16,32]{1,0:T(8,128)}, f32[16,32]{1,0:T(8,128)S(1)}, u32[]{:S(2)}) copy-start(f32[16,32]{1,0:T(8,128)S(1)} %get-tuple-element.16) | copy-start | bytes 6148
  31.4 27.8 %copy-start.63 = (f32[16,32]{1,0:T(8,128)}, f32[16,32]{1,0:T(8,128)S(1)}, u32[]{:S(2)}) copy-start(f32[16,32]{1,0:T(8,128)S(1)} %get-tuple-element.49) | copy-start | bytes 6148
  59.2 45.4 %copy-start = (f32[16,32,3456]{2,1,0:T(8,128)}, f32[16,32,3456]{2,1,0:T(8,128)S(1)}, u32[]{:S(2)}) copy-start(f32[16,32,3456]{2,1,0:T(8,128)S(1)} %select_select_fusion.1) | copy-start | bytes 21233668
  59.4 22.6 %collective-permute-start.1 = (f32[2,32,3456]{2,1,0:T(8,128)S(1)}, f32[2,32,3456]{2,1,0:T(8,128)S(1)}, u32[]{:S(2)}, u32[]{:S(2)}) collective-permute-start(f32[2,32,3456]{2,1,0:T(8,128)S(1)} %get-tuple-element.28), channel_id=1, source_target_pairs={{16,0},{0,16},{17,1},{1,17},{18,2},{2,18},{19,3},{3,19},{20,4},{4,... | collective-permute-start | bytes 2654216 | tf_op jit(solution)/shard_map/ppermute | solution.py:29
  61.0 38.7 %collective-permute-start = (f32[2,32,3456]{2,1,0:T(8,128)S(1)}, f32[2,32,3456]{2,1,0:T(8,128)S(1)}, u32[]{:S(2)}, u32[]{:S(2)}) collective-permute-start(f32[2,32,3456]{2,1,0:T(8,128)S(1)} %get-tuple-element.27), channel_id=1, source_target_pairs={{0,16},{16,0},{1,17},{17,1},{2,18},{18,2},{3,19},{19,3},{4,20},{20... | collective-permute-start | bytes 2654216 | tf_op jit(solution)/shard_map/ppermute | solution.py:28
  62.2 67.3 %copy-start.39 = (f32[3456]{0:T(1024)}, f32[3456]{0:T(1024)S(1)}, u32[]{:S(2)}) copy-start(f32[3456]{0:T(1024)S(1)} %get-tuple-element.62) | copy-start | bytes 41476
  62.2 67.3 %copy-start.41 = (f32[3456]{0:T(1024)}, f32[3456]{0:T(1024)S(1)}, u32[]{:S(2)}) copy-start(f32[3456]{0:T(1024)S(1)} %get-tuple-element.63) | copy-start | bytes 41476
  82.0 57.9 %copy-start.5 = (f32[2,32,3456]{2,1,0:T(8,128)}, f32[2,32,3456]{2,1,0:T(8,128)S(1)}, u32[]{:S(2)}) copy-start(f32[2,32,3456]{2,1,0:T(8,128)S(1)} %collective-permute-done.1) | copy-start | bytes 2654212
  99.7 40.2 %copy-start.7 = (f32[2,32,3456]{2,1,0:T(8,128)}, f32[2,32,3456]{2,1,0:T(8,128)S(1)}, u32[]{:S(2)}) copy-start(f32[2,32,3456]{2,1,0:T(8,128)S(1)} %collective-permute-done) | copy-start | bytes 2654212
  100.1 38.1 %collective-permute-start.3 = (f32[20,2,3456]{2,0,1:T(8,128)S(1)}, f32[20,2,3456]{2,0,1:T(8,128)S(1)}, u32[]{:S(2)}, u32[]{:S(2)}) collective-permute-start(f32[20,2,3456]{2,0,1:T(8,128)S(1)} %copy.44), channel_id=1, source_target_pairs={{4,0},{8,4},{12,8},{0,12},{5,1},{9,5},{13,9},{1,13},{6,2},{10,6},{... | collective-permute-start | bytes 1658888 | tf_op jit(solution)/shard_map/ppermute | solution.py:29
  104.7 33.8 %collective-permute-start.2 = (f32[20,2,3456]{2,0,1:T(8,128)}, f32[20,2,3456]{2,0,1:T(8,128)}, u32[]{:S(2)}, u32[]{:S(2)}) collective-permute-start(f32[20,2,3456]{2,0,1:T(8,128)} %copy.42), channel_id=1, source_target_pairs={{0,4},{4,8},{8,12},{12,0},{1,5},{5,9},{9,13},{13,1},{2,6},{6,10},{... | collective-permute-start | bytes 1658888 | tf_op jit(solution)/shard_map/ppermute | solution.py:28
  145.7 23.0 %slice-start = ((s8[7077888]{0:T(1024)(128)(4,1)}), s8[2883584]{0:T(1024)(128)(4,1)S(1)}, s32[]{:S(2)}) async-start(s8[7077888]{0:T(1024)(128)(4,1)} %bitcast.82), calls=%async_computation | async-start | bytes 5767168
  156.4 12.3 %copy-start.8 = (f32[2,32,3456]{2,1,0:T(8,128)S(1)}, f32[2,32,3456]{2,1,0:T(8,128)}, u32[]{:S(2)}) copy-start(f32[2,32,3456]{2,1,0:T(8,128)} %copy-done.7) | copy-start | bytes 2654212
  156.4 12.4 %copy-start.35 = (f32[3456]{0:T(1024)S(1)}, f32[3456]{0:T(1024)}, u32[]{:S(2)}) copy-start(f32[3456]{0:T(1024)} %get-tuple-element.60) | copy-start | bytes 41476
  156.4 12.4 %copy-start.37 = (f32[3456]{0:T(1024)S(1)}, f32[3456]{0:T(1024)}, u32[]{:S(2)}) copy-start(f32[3456]{0:T(1024)} %get-tuple-element.61) | copy-start | bytes 41476
  156.4 28.4 %slice-start.6 = ((s8[7077888]{0:T(1024)(128)(4,1)}), s8[4194304]{0:T(1024)(128)(4,1)S(1)}, s32[]{:S(2)}) async-start(s8[7077888]{0:T(1024)(128)(4,1)} %bitcast.88), calls=%async_computation.6 | async-start | bytes 8388608
  168.8 16.0 %slice-start.7 = ((s8[7077888]{0:T(1024)(128)(4,1)}), s8[2883584]{0:T(1024)(128)(4,1)S(1)}, s32[]{:S(2)}) async-start(s8[7077888]{0:T(1024)(128)(4,1)} %bitcast.88), calls=%async_computation.7 | async-start | bytes 5767168
  168.8 16.0 %copy-start.16 = (f32[3456]{0:T(1024)S(1)}, f32[3456]{0:T(1024)}, u32[]{:S(2)}) copy-start(f32[3456]{0:T(1024)} %copy-done.15) | copy-start | bytes 41476
  168.8 16.0 %copy-start.20 = (f32[3456]{0:T(1024)S(1)}, f32[3456]{0:T(1024)}, u32[]{:S(2)}) copy-start(f32[3456]{0:T(1024)} %copy-done.19) | copy-start | bytes 41476
  168.8 16.0 %copy-start.24 = (f32[3456]{0:T(1024)S(1)}, f32[3456]{0:T(1024)}, u32[]{:S(2)}) copy-start(f32[3456]{0:T(1024)} %copy-done.23) | copy-start | bytes 41476
  168.8 16.0 %copy-start.28 = (f32[3456]{0:T(1024)S(1)}, f32[3456]{0:T(1024)}, u32[]{:S(2)}) copy-start(f32[3456]{0:T(1024)} %copy-done.27) | copy-start | bytes 41476
  168.9 16.0 %copy-start.32 = (f32[3456]{0:T(1024)S(1)}, f32[3456]{0:T(1024)}, u32[]{:S(2)}) copy-start(f32[3456]{0:T(1024)} %copy-done.31) | copy-start | bytes 41476
  168.9 16.0 %copy-start.44 = (f32[16,32]{1,0:T(8,128)S(1)}, f32[16,32]{1,0:T(8,128)}, u32[]{:S(2)}) copy-start(f32[16,32]{1,0:T(8,128)} %copy-done.43) | copy-start | bytes 6148
  168.9 16.0 %copy-start.46 = (f32[16,32]{1,0:T(8,128)S(1)}, f32[16,32]{1,0:T(8,128)}, u32[]{:S(2)}) copy-start(f32[16,32]{1,0:T(8,128)} %copy-done.45) | copy-start | bytes 6148
  168.9 16.0 %copy-start.48 = (f32[16,32]{1,0:T(8,128)S(1)}, f32[16,32]{1,0:T(8,128)}, u32[]{:S(2)}) copy-start(f32[16,32]{1,0:T(8,128)} %copy-done.47) | copy-start | bytes 6148
  168.9 16.0 %copy-start.50 = (f32[16,32]{1,0:T(8,128)S(1)}, f32[16,32]{1,0:T(8,128)}, u32[]{:S(2)}) copy-start(f32[16,32]{1,0:T(8,128)} %copy-done.49) | copy-start | bytes 6148
  168.9 16.0 %copy-start.52 = (f32[16,32]{1,0:T(8,128)S(1)}, f32[16,32]{1,0:T(8,128)}, u32[]{:S(2)}) copy-start(f32[16,32]{1,0:T(8,128)} %copy-done.51) | copy-start | bytes 6148
  168.9 16.0 %copy-start.54 = (f32[16,32]{1,0:T(8,128)S(1)}, f32[16,32]{1,0:T(8,128)}, u32[]{:S(2)}) copy-start(f32[16,32]{1,0:T(8,128)} %copy-done.53) | copy-start | bytes 6148
  168.9 16.0 %copy-start.56 = (f32[16,32]{1,0:T(8,128)S(1)}, f32[16,32]{1,0:T(8,128)}, u32[]{:S(2)}) copy-start(f32[16,32]{1,0:T(8,128)} %copy-done.55) | copy-start | bytes 6148
  168.9 16.0 %copy-start.58 = (f32[16,32]{1,0:T(8,128)S(1)}, f32[16,32]{1,0:T(8,128)}, u32[]{:S(2)}) copy-start(f32[16,32]{1,0:T(8,128)} %copy-done.57) | copy-start | bytes 6148
  168.9 16.0 %copy-start.60 = (f32[16,32]{1,0:T(8,128)S(1)}, f32[16,32]{1,0:T(8,128)}, u32[]{:S(2)}) copy-start(f32[16,32]{1,0:T(8,128)} %copy-done.59) | copy-start | bytes 6148
  169.0 16.0 %copy-start.62 = (f32[16,32]{1,0:T(8,128)S(1)}, f32[16,32]{1,0:T(8,128)}, u32[]{:S(2)}) copy-start(f32[16,32]{1,0:T(8,128)} %copy-done.61) | copy-start | bytes 6148
  169.0 16.0 %copy-start.64 = (f32[16,32]{1,0:T(8,128)S(1)}, f32[16,32]{1,0:T(8,128)}, u32[]{:S(2)}) copy-start(f32[16,32]{1,0:T(8,128)} %copy-done.63) | copy-start | bytes 6148
  169.0 16.0 %copy-start.66 = (pred[16,32]{1,0:T(8,128)(4,1)S(1)}, pred[16,32]{1,0:T(8,128)(4,1)}, u32[]{:S(2)}) copy-start(pred[16,32]{1,0:T(8,128)(4,1)} %copy-done.65) | copy-start | bytes 1540
  169.0 16.0 %copy-start.69 = (pred[16,32]{1,0:T(8,128)(4,1)S(1)}, pred[16,32]{1,0:T(8,128)(4,1)}, u32[]{:S(2)}) copy-start(pred[16,32]{1,0:T(8,128)(4,1)} %copy-done.68) | copy-start | bytes 1540
  203.0 25.1 %copy-start.72 = (f32[16,32]{1,0:T(8,128)S(1)}, f32[16,32]{1,0:T(8,128)}, u32[]{:S(2)}) copy-start(f32[16,32]{1,0:T(8,128)} %param.5) | copy-start | bytes 6148
  203.0 25.1 %copy-start.17 = (f32[3456]{0:T(1024)S(1)}, f32[3456]{0:T(1024)}, u32[]{:S(2)}) copy-start(f32[3456]{0:T(1024)} %copy-done.15) | copy-start | bytes 41476
  203.0 25.1 %copy-start.21 = (f32[3456]{0:T(1024)S(1)}, f32[3456]{0:T(1024)}, u32[]{:S(2)}) copy-start(f32[3456]{0:T(1024)} %copy-done.19) | copy-start | bytes 41476
  203.0 25.2 %copy-start.25 = (f32[3456]{0:T(1024)S(1)}, f32[3456]{0:T(1024)}, u32[]{:S(2)}) copy-start(f32[3456]{0:T(1024)} %copy-done.23) | copy-start | bytes 41476
  203.0 41.9 %copy-start.29 = (f32[3456]{0:T(1024)S(1)}, f32[3456]{0:T(1024)}, u32[]{:S(2)}) copy-start(f32[3456]{0:T(1024)} %copy-done.27) | copy-start | bytes 41476
  203.0 41.9 %copy-start.33 = (f32[3456]{0:T(1024)S(1)}, f32[3456]{0:T(1024)}, u32[]{:S(2)}) copy-start(f32[3456]{0:T(1024)} %copy-done.31) | copy-start | bytes 41476
  203.0 41.9 %copy-start.67 = (pred[16,32]{1,0:T(8,128)(4,1)S(1)}, pred[16,32]{1,0:T(8,128)(4,1)}, u32[]{:S(2)}) copy-start(pred[16,32]{1,0:T(8,128)(4,1)} %copy-done.65) | copy-start | bytes 1540
  203.0 41.9 %copy-start.70 = (pred[16,32]{1,0:T(8,128)(4,1)S(1)}, pred[16,32]{1,0:T(8,128)(4,1)}, u32[]{:S(2)}) copy-start(pred[16,32]{1,0:T(8,128)(4,1)} %copy-done.68) | copy-start | bytes 1540
  255.4 45.6 %copy-start.2 = (f32[16,32,3456]{2,1,0:T(8,128)}, f32[16,32,3456]{2,1,0:T(8,128)S(1)}, u32[]{:S(2)}) copy-start(f32[16,32,3456]{2,1,0:T(8,128)S(1)} %select_select_fusion) | copy-start | bytes 21233668
  255.5 22.6 %collective-permute-start.5 = (f32[2,32,3456]{2,1,0:T(8,128)S(1)}, f32[2,32,3456]{2,1,0:T(8,128)S(1)}, u32[]{:S(2)}, u32[]{:S(2)}) collective-permute-start(f32[2,32,3456]{2,1,0:T(8,128)S(1)} %get-tuple-element.26), channel_id=1, source_target_pairs={{16,0},{0,16},{17,1},{1,17},{18,2},{2,18},{19,3},{3,19},{20,4},{4,... | collective-permute-start | bytes 2654216 | tf_op jit(solution)/shard_map/ppermute | solution.py:29
  257.1 38.7 %collective-permute-start.4 = (f32[2,32,3456]{2,1,0:T(8,128)S(1)}, f32[2,32,3456]{2,1,0:T(8,128)S(1)}, u32[]{:S(2)}, u32[]{:S(2)}) collective-permute-start(f32[2,32,3456]{2,1,0:T(8,128)S(1)} %get-tuple-element.25), channel_id=1, source_target_pairs={{0,16},{16,0},{1,17},{17,1},{2,18},{18,2},{3,19},{19,3},{4,20},{20... | collective-permute-start | bytes 2654216 | tf_op jit(solution)/shard_map/ppermute | solution.py:28
  278.1 58.3 %copy-start.9 = (f32[2,32,3456]{2,1,0:T(8,128)}, f32[2,32,3456]{2,1,0:T(8,128)S(1)}, u32[]{:S(2)}) copy-start(f32[2,32,3456]{2,1,0:T(8,128)S(1)} %collective-permute-done.5) | copy-start | bytes 2654212
  295.8 40.7 %copy-start.11 = (f32[2,32,3456]{2,1,0:T(8,128)}, f32[2,32,3456]{2,1,0:T(8,128)S(1)}, u32[]{:S(2)}) copy-start(f32[2,32,3456]{2,1,0:T(8,128)S(1)} %collective-permute-done.4) | copy-start | bytes 2654212
  296.3 38.5 %collective-permute-start.7 = (f32[20,2,3456]{2,0,1:T(8,128)S(1)}, f32[20,2,3456]{2,0,1:T(8,128)S(1)}, u32[]{:S(2)}, u32[]{:S(2)}) collective-permute-start(f32[20,2,3456]{2,0,1:T(8,128)S(1)} %copy.51), channel_id=1, source_target_pairs={{4,0},{8,4},{12,8},{0,12},{5,1},{9,5},{13,9},{1,13},{6,2},{10,6},{... | collective-permute-start | bytes 1658888 | tf_op jit(solution)/shard_map/ppermute | solution.py:29
  301.0 34.1 %collective-permute-start.6 = (f32[20,2,3456]{2,0,1:T(8,128)}, f32[20,2,3456]{2,0,1:T(8,128)}, u32[]{:S(2)}, u32[]{:S(2)}) collective-permute-start(f32[20,2,3456]{2,0,1:T(8,128)} %copy.49), channel_id=1, source_target_pairs={{0,4},{4,8},{8,12},{12,0},{1,5},{5,9},{9,13},{13,1},{2,6},{6,10},{... | collective-permute-start | bytes 1658888 | tf_op jit(solution)/shard_map/ppermute | solution.py:28
  342.4 23.0 %slice-start.2 = ((s8[7077888]{0:T(1024)(128)(4,1)}), s8[2883584]{0:T(1024)(128)(4,1)S(1)}, s32[]{:S(2)}) async-start(s8[7077888]{0:T(1024)(128)(4,1)} %bitcast.84), calls=%async_computation.2 | async-start | bytes 5767168
  353.0 12.3 %copy-start.12 = (f32[2,32,3456]{2,1,0:T(8,128)S(1)}, f32[2,32,3456]{2,1,0:T(8,128)}, u32[]{:S(2)}) copy-start(f32[2,32,3456]{2,1,0:T(8,128)} %copy-done.11) | copy-start | bytes 2654212
  353.0 12.4 %copy-start.36 = (f32[3456]{0:T(1024)S(1)}, f32[3456]{0:T(1024)}, u32[]{:S(2)}) copy-start(f32[3456]{0:T(1024)} %get-tuple-element.60) | copy-start | bytes 41476
  353.0 12.4 %copy-start.38 = (f32[3456]{0:T(1024)S(1)}, f32[3456]{0:T(1024)}, u32[]{:S(2)}) copy-start(f32[3456]{0:T(1024)} %get-tuple-element.61) | copy-start | bytes 41476
  353.0 19.7 %slice-start.4 = ((s8[7077888]{0:T(1024)(128)(4,1)}), s8[4194304]{0:T(1024)(128)(4,1)S(1)}, s32[]{:S(2)}) async-start(s8[7077888]{0:T(1024)(128)(4,1)} %bitcast.86), calls=%async_computation.4 | async-start | bytes 8388608
  (26 other events, 235.8 us)
where the time goes:
time: 397 us; the launch traced here: 390 us
  other arithmetic  215 us (54%)
  waiting for transfers between devices  75.6 us (19%)
  blocking collectives  45 us (11%)
  matrix products  30.6 us (8%)
  starting transfers between devices  11.7 us (3%)
  local copies, waits for them, and re-layouts  10.5 us (3%)
    mul x4, other arithmetic, minmod(): 0.5 * (jnp.sign(left) + jnp.sign(right))  45.7 us
    sub x4, other arithmetic, sweep_strip(): lax.slice_in_dim(strip, 1, length, axis=axis)  42.4 us
    ppermute x4, waiting for transfers between devices, extended(): after = lax.ppermute(initial, axis, down)  40.3 us
    add x4, other arithmetic, sweep_strip(): forward * (lax.slice_in_dim(cells, 0, length - 3, axis=axis) + 0.5 * lax....  40.3 us
    ppermute x4, waiting for transfers between devices, extended(): before = lax.ppermute(last, axis, up)  35.3 us
    sub x2, other arithmetic, transport(): return centre - CLOCK_ADVANCE * change  31.7 us
    dot_general x2, matrix products, moments(): jnp.einsum('kv,xyv->kxy', basis, present_state, precision=lax.Precision.H...  30.6 us
    psum x2, blocking collectives, moments(): quadrature_totals = lax.psum(local, 'vel')  24.1 us
  transfers between devices with their start and end apart: 8, of which 4 were waited for; matrix products, arithmetic and copies ran while one was open for 18% of the time, Pallas kernels for 0%

commit v1 on v0

v1 whole, which is shorter than its diff:
```python
import functools
import math

import jax
import jax.numpy as jnp
from jax import lax
from jax.experimental import pallas as pl
from jax.experimental.pallas import tpu as pltpu
from jax.sharding import PartitionSpec as P

NVX = 24
STEPS = 2
VEL_LIMIT = 4.8
DT = 0.09
SPACING = 2.0 * VEL_LIMIT / NVX
HALF = 0.5 * SPACING
WEIGHT = SPACING**3
LANES = 128
PITCH = 48
TOP = 8
MESH = pl.DeviceIdType.MESH
F32 = jnp.float32
BF16 = jnp.bfloat16


def tables(index, valid):
    p = [index % NVX, index // NVX % NVX, index // (NVX * NVX)]
    m = [(2 * (q // 2) + 1) * (2 * (q % 2) - 1) for q in p]
    x, y, z = m
    sq = x * x + y * y + z * z
    quads = [x * x, y * y, z * z, x * y, x * z, y * z]
    cubes = [x * sq, y * sq, z * sq]
    q_hi = [(v + 8) // 16 * 16 for v in quads]
    c_hi = [(v + 128) // 256 * 256 for v in cubes]
    q_lo = [a - b for a, b in zip(quads, q_hi)]
    c_lo = [a - b for a, b in zip(cubes, c_hi)]
    one, zero = jnp.ones_like(x), jnp.zeros_like(x)
    rows = [one, x, y, z] + q_hi + c_hi + [zero] * 3 + [zero] * 4 + q_lo + c_lo + [zero] * 3
    phi = jnp.stack([jnp.where(valid, r, 0).astype(BF16) for r in rows], axis=1)
    speeds = [
        (x > 0).astype(F32),
        (y > 0).astype(F32),
        DT * HALF * jnp.abs(x).astype(F32),
        DT * HALF * jnp.abs(y).astype(F32),
    ]
    lane = jnp.stack(speeds + [jnp.zeros_like(speeds[0])] * 4, axis=1)
    return phi, lane


def coefficients(s, kind, kn):
    n = s[0]
    rho = WEIGHT * n
    u = [HALF * s[i + 1] / n for i in range(3)]
    h2 = HALF * HALF
    mom = [h2 * s[4 + i] for i in range(6)]
    xx, yy, zz, xy, xz, yz = mom
    energy = xx + yy + zz
    usq = u[0] * u[0] + u[1] * u[1] + u[2] * u[2]
    temp = (energy / n - usq) / 3.0
    second = [[xx, xy, xz], [xy, yy, yz], [xz, yz, zz]]
    q = []
    for i in range(3):
        third = h2 * HALF * s[10 + i]
        mixed = u[0] * second[i][0] + u[1] * second[i][1] + u[2] * second[i][2]
        q.append(0.5 * WEIGHT * (third - 2.0 * mixed - u[i] * energy + 2.0 * n * u[i] * usq))
    keep = jnp.exp(-DT * rho * jnp.sqrt(temp) / kn)
    inv = 1.0 / temp
    tau = 2.0 * math.pi * temp
    front = rho / (tau * jnp.sqrt(tau)) * (1.0 - keep)
    kappa = (1.0 / 3.0) / (5.0 * rho * temp * temp)
    b = usq * inv - 5.0
    uq = u[0] * q[0] + u[1] * q[1] + u[2] * q[2]
    fk = front * kappa
    wall, inflow = kind == 1, kind == 2
    gas = jnp.logical_not(jnp.logical_or(wall, inflow))
    zero = jnp.zeros_like(n)

    def pick(g, w, i):
        return jnp.where(wall, w, jnp.where(inflow, i, g))

    norm = (2.0 * math.pi) ** -1.5
    arg_sq = pick(-0.5 * h2 * inv, zero - 0.5 * h2, zero - 0.5 * h2)
    arg = [
        pick(-0.5 * usq * inv, zero, zero - 0.125),
        pick(HALF * u[0] * inv, zero, zero + 0.5 * HALF),
        pick(HALF * u[1] * inv, zero, zero),
        pick(HALF * u[2] * inv, zero, zero),
    ] + [arg_sq] * 3 + [zero] * 9
    poly = [pick(front - fk * uq * b, rho * norm, zero + 12.0 * norm)]
    rest = [fk * HALF * (b * q[i] + 2.0 * uq * u[i] * inv) for i in range(3)]
    rest += [-fk * h2 * inv * (2.0 * q[i] * u[i] + uq) for i in range(3)]
    rest += [
        -2.0 * fk * h2 * inv * (q[i] * u[j] + q[j] * u[i]) for i, j in ((0, 1), (0, 2), (1, 2))
    ]
    rest += [fk * h2 * HALF * inv * q[i] for i in range(3)]
    poly += [jnp.where(gas, r, 0.0) for r in rest] + [zero] * 3
    return arg, poly, jnp.where(gas, keep, 0.0)


def pieces(rows):
    whole = jnp.concatenate(rows, axis=0)
    both = jnp.concatenate([whole, whole], axis=0)
    first = both.astype(BF16).astype(F32)
    left = both - first
    second = left.astype(BF16).astype(F32)
    third = left - second
    full = jnp.concatenate([first, second, third, jnp.zeros_like(first)], axis=0)
    return full.T.astype(BF16)


def minmod_pair(mid, a, b):
    lo, hi = jnp.minimum(mid, 0.0), jnp.maximum(mid, 0.0)
    return jnp.minimum(jnp.maximum(a, lo), hi) - jnp.minimum(jnp.maximum(b, lo), hi)


def upwind(pos, far_lo, lo, mid, hi, far_hi):
    before = jnp.where(pos, lo, hi)
    after = jnp.where(pos, hi, lo)
    far = jnp.where(pos, far_lo, far_hi)
    step = mid - before
    return step + 0.5 * minmod_pair(step, after - mid, before - far)


def kernel(
    sizes, group, dist, phi_ref, lane_ref, kind_ref, kn_ref, out,
    f, g, c_send, y_send, xh, yh, acc, arg_c, poly_c, keep_c, ps,
    in_sem, out_sem, send_sem, recv_sem, ps_send, ps_recv,
):
    nsx, nsy, nvel = sizes
    ncol, nx, ny = f.shape[:3]
    cells = nx * ny
    groups = ncol // group
    x_size, y_size, v_size = nsx, nsy, nvel
    ix, iy, iv = lax.axis_index("sx"), lax.axis_index("sy"), lax.axis_index("vel")
    x_up, x_down = lax.rem(ix + 1, x_size), lax.rem(ix + x_size - 1, x_size)
    y_up, y_down = lax.rem(iy + 1, y_size), lax.rem(iy + y_size - 1, y_size)

    def in_copy(j):
        return pltpu.make_async_copy(
            dist.at[:, :, pl.ds(pl.multiple_of(j * LANES, LANES), LANES)],
            f.at[j],
            in_sem.at[j],
        )

    def out_copy(j):
        return pltpu.make_async_copy(
            f.at[j],
            out.at[:, :, pl.ds(pl.multiple_of(j * LANES, LANES), LANES)],
            out_sem.at[j],
        )

    @pl.loop(0, ncol)
    def _(j):
        in_copy(j).start()

    partners = [{"vel": lax.rem(iv + o, v_size)} for o in range(1, nvel)]
    partners += [{"sx": x_up}] + ([{"sx": x_down}] if nsx > 2 else [])
    partners += [{"sy": y_up}] + ([{"sy": y_down}] if nsy > 2 else [])
    barrier = pltpu.get_barrier_semaphore()
    for who in partners:
        pl.semaphore_signal(barrier, inc=1, device_id=who, device_id_type=MESH)
    pl.semaphore_wait(barrier, len(partners))

    def face(slab):
        return pl.ds(slab * PITCH + TOP, ny)

    def halo_copies(step, k):
        cols = pl.ds(k * group, group)

        def remote(n, src, dst, who):
            return pltpu.make_async_remote_copy(
                src_ref=src, dst_ref=dst,
                send_sem=send_sem.at[step, k, n], recv_sem=recv_sem.at[step, k, n],
                device_id=who, device_id_type=MESH,
            )

        copies = [
            remote(0, g.at[cols, face(nx + 1)], xh.at[step, cols, 1], {"sx": x_up}),
            remote(1, g.at[cols, face(2)], xh.at[step, cols, 2], {"sx": x_down}),
            remote(2, c_send.at[cols], xh.at[step, cols, 0], {"sx": x_up}),
            remote(3, y_send.at[cols, 1], yh.at[step, cols, 0], {"sy": y_up}),
            remote(4, y_send.at[cols, 0], yh.at[step, cols, 1], {"sy": y_down}),
        ]
        if nsx > 2:
            copies.append(remote(5, c_send.at[cols], xh.at[step, cols, 3], {"sx": x_down}))
        return copies

    def add_moments(j):
        phi = phi_ref[j]
        wide = jnp.concatenate([phi, phi, phi, phi], axis=0)
        both = jnp.concatenate([wide, wide], axis=1)
        for r in range(0, cells, 128):
            val = f[j, r // ny : (r + 128) // ny].reshape(128, LANES)
            hi = val.astype(BF16)
            lo = (val - hi.astype(F32)).astype(BF16)
            acc[r : r + 128, :] += lax.dot_general(
                jnp.concatenate([hi, lo], axis=1), both,
                (((1,), (1,)), ((), ())), preferred_element_type=F32,
            )

    def exchange(step):
        local = acc[...].T
        ps[step, iv] = local[0:16] + local[16:32]
        copies = []
        for o in range(1, nvel):
            copy = pltpu.make_async_remote_copy(
                src_ref=ps.at[step, iv], dst_ref=ps.at[step, iv],
                send_sem=ps_send.at[step, o], recv_sem=ps_recv.at[step, o],
                device_id={"vel": lax.rem(iv + o, v_size)}, device_id_type=MESH,
            )
            copy.start()
            copies.append(copy)
        for copy in copies:
            copy.wait()
        total = ps[step, 0]
        for v in range(1, nvel):
            total = total + ps[step, v]
        rows = [total[i : i + 1] for i in range(13)]
        arg, poly, keep = coefficients(rows, kind_ref[...], kn_ref[...])
        arg_c[...] = pieces(arg)
        poly_c[...] = pieces(poly)
        keep_c[...] = jnp.broadcast_to(keep, (LANES, cells)).T

    def relax(j):
        phi = phi_ref[j]
        wide = jnp.concatenate([phi, phi, phi, phi], axis=0)
        for r in range(0, cells, 128):
            rows = pl.ds(r, 128)
            arg = jnp.dot(arg_c[rows, :], wide, preferred_element_type=F32)
            poly = jnp.dot(poly_c[rows, :], wide, preferred_element_type=F32)
            val = f[j, r // ny : (r + 128) // ny].reshape(128, LANES)
            new = val * keep_c[rows, :] + jnp.exp(arg) * poly
            for i in range(128 // ny):
                slab = r // ny + i + 2
                g[j, face(slab), :] = new[i * ny : (i + 1) * ny]
        pos = jnp.broadcast_to(lane_ref[j, 0:1, :], (ny, LANES)) > 0.0
        c_send[j] = jnp.where(pos, g[j, face(nx), :], g[j, face(3), :])
        for side, first in ((0, 0), (1, ny - 2)):
            for layer in range(2):
                y_send[j, side, layer * nx : (layer + 1) * nx, :] = g[
                    j, pl.ds(2 * PITCH + TOP + first + layer, nx, stride=PITCH), :
                ]

    def transport(step, j):
        lanes = lane_ref[j]
        pos_x = jnp.broadcast_to(lanes[0:1], (ny, LANES)) > 0.0
        pos_y = jnp.broadcast_to(lanes[1:2], (ny, LANES)) > 0.0
        rate_x = jnp.broadcast_to(lanes[2:3], (ny, LANES))
        rate_y = jnp.broadcast_to(lanes[3:4], (ny, LANES))
        far = xh[step, j, 0]
        g[j, face(0), :] = far
        g[j, face(1), :] = xh[step, j, 1]
        g[j, face(nx + 2), :] = xh[step, j, 2]
        g[j, face(nx + 3), :] = far if nsx == 2 else xh[step, j, 3]
        for side, first in ((0, -2), (1, ny)):
            for layer in range(2):
                g[j, pl.ds(2 * PITCH + TOP + first + layer, nx, stride=PITCH), :] = yh[
                    step, j, side, layer * nx : (layer + 1) * nx, :
                ]
        for x in range(nx):
            base = (x + 2) * PITCH + TOP
            mid = g[j, pl.ds(base, ny), :]
            along_x = [g[j, pl.ds(base + d * PITCH, ny), :] for d in (-2, -1, 1, 2)]
            along_y = [g[j, pl.ds(base + d, ny), :] for d in (-2, -1, 1, 2)]
            div_x = upwind(pos_x, along_x[0], along_x[1], mid, along_x[2], along_x[3])
            div_y = upwind(pos_y, along_y[0], along_y[1], mid, along_y[2], along_y[3])
            f[j, x] = mid - (rate_x * div_x + rate_y * div_y)

    acc[...] = jnp.zeros_like(acc)

    @pl.loop(0, ncol)
    def _(j):
        in_copy(j).wait()
        add_moments(j)

    for step in range(STEPS):
        last = step == STEPS - 1
        exchange(step)

        @pl.loop(0, groups)
        def _(k):
            @pl.loop(0, group)
            def _(i):
                relax(k * group + i)

            for copy in halo_copies(step, k):
                copy.start()

        if not last:
            acc[...] = jnp.zeros_like(acc)

        @pl.loop(0, groups)
        def _(k):
            for copy in halo_copies(step, k):
                copy.wait()

            @pl.loop(0, group)
            def _(i):
                j = k * group + i
                transport(step, j)
                if last:
                    out_copy(j).start()
                else:
                    add_moments(j)

    @pl.loop(0, ncol)
    def _(j):
        out_copy(j).wait()


def body(sizes, distribution, cell_kind, local_knudsen):
    nx, ny, count = distribution.shape
    ncol = -(-count // LANES)
    width = ncol * LANES
    offset = jnp.arange(width, dtype=jnp.int32).reshape(ncol, LANES)
    phi, lane = tables(lax.axis_index("vel") * count + offset, offset < count)
    padded = distribution
    if width != count:
        padded = jnp.pad(distribution, ((0, 0), (0, 0), (0, width - count)))
    group = 3 if ncol % 3 == 0 else 1
    groups, cells = ncol // group, nx * ny
    nsx, nsy, nvel = sizes
    xcopies = 3 if nsx == 2 else 4
    dma = pltpu.SemaphoreType.DMA
    any_spec = pl.BlockSpec(memory_space=pl.ANY)
    vmem = pl.BlockSpec(memory_space=pltpu.VMEM)
    result = pl.pallas_call(
        functools.partial(kernel, sizes, group),
        out_shape=jax.ShapeDtypeStruct((nx, ny, width), F32),
        in_specs=[any_spec, vmem, vmem, vmem, vmem],
        out_specs=any_spec,
        scratch_shapes=[
            pltpu.VMEM((ncol, nx, ny, LANES), F32),
            pltpu.VMEM((ncol, (nx + 4) * PITCH, LANES), F32),
            pltpu.VMEM((ncol, ny, LANES), F32),
            pltpu.VMEM((ncol, 2, 2 * nx, LANES), F32),
            pltpu.VMEM((STEPS, ncol, xcopies, ny, LANES), F32),
            pltpu.VMEM((STEPS, ncol, 2, 2 * nx, LANES), F32),
            pltpu.VMEM((cells, LANES), F32),
            pltpu.VMEM((cells, LANES), BF16),
            pltpu.VMEM((cells, LANES), BF16),
            pltpu.VMEM((cells, LANES), F32),
            pltpu.VMEM((STEPS, nvel, 16, cells), F32),
            dma((ncol,)),
            dma((ncol,)),
            dma((STEPS, groups, xcopies + 2)),
            dma((STEPS, groups, xcopies + 2)),
            dma((STEPS, nvel)),
            dma((STEPS, nvel)),
        ],
        compiler_params=pltpu.CompilerParams(
            collective_id=0, has_side_effects=True, vmem_limit_bytes=56 * 2**20
        ),
    )(padded, phi, lane, cell_kind.reshape(1, cells), local_knudsen.reshape(1, cells))
    return result[..., :count] if width != count else result


def solution(mesh):
    sizes = (mesh.shape["sx"], mesh.shape["sy"], mesh.shape["vel"])
    return jax.shard_map(
        functools.partial(body, sizes),
        mesh=mesh,
        in_specs=(P("sx", "sy", "vel"), P("sx", "sy"), P("sx", "sy")),
        out_specs=P("sx", "sy", "vel"),
        check_vma=False,
    )
```

time: 397 us -> 108 us (0.27); the launches traced: 390 us -> 108 us
  other arithmetic: 215 us -> 7.79 us
  Pallas kernels: 0 us -> 87.1 us
  waiting for transfers between devices: 75.6 us -> 0 us
  blocking collectives: 45 us -> 0 us
  matrix products: 30.6 us -> 0 us
  starting transfers between devices: 11.7 us -> 0 us
    pallas_call x0 -> x1, Pallas kernels: none -> 87.1 us  [body(): pl.pallas_call(functools.partial(kernel, sizes, group), out_shape=jax.Sha...]
    ppermute x8 -> x0, waiting for transfers between devices: 75.6 us -> none  [the longest x4 40.3 us: extended(): after = lax.ppermute(initial, axis, down)]
    sub x6 -> x0, other arithmetic: 74.1 us -> none  [the longest x4 42.4 us: sweep_strip(): lax.slice_in_dim(strip, 1, length, axis=axis)]
    mul x13 -> x1, other arithmetic: 47 us -> 0.43 us  [tables(): DT * HALF * jnp.abs(y).astype(F32)]
    psum x4 -> x0, blocking collectives: 45 us -> none  [the longest x2 24.1 us: moments(): quadrature_totals = lax.psum(local, 'vel')]
    add x4 -> x0, other arithmetic: 40.3 us -> none  [sweep_strip(): forward * (lax.slice_in_dim(cells, 0, length - 3, axis=axis) + 0.5 * lax....]
    dot_general x2 -> x0, matrix products: 30.6 us -> none  [moments(): jnp.einsum('kv,xyv->kxy', basis, present_state, precision=lax.Precision.H...]
    select_n x2 -> x0, other arithmetic: 20.8 us -> none  [relax(): jnp.where(widen_last_index(cell_kind == 1), wall, jnp.where(widen_last_in...]
  transfers between devices with their start and end apart: 8 -> 0, of which waited for: 4 -> 0; matrix products, arithmetic and copies ran while one was open for 18% -> 0% of each run, Pallas kernels for 0% -> 0%
where the time goes in v1:
time: 108 us
  Pallas kernels  87.1 us (81%)
  local copies, waits for them, and re-layouts  13.1 us (12%)
  other arithmetic  7.79 us (7%)
    pallas_call x1, Pallas kernels, body(): pl.pallas_call(functools.partial(kernel, sizes, group), out_shape=jax.Sha...  87.1 us
    convert_element_type x11, other arithmetic, tables(): phi = jnp.stack([jnp.where(valid, r, 0).astype(BF16) for r in rows], axis=1)  6.95 us
    unnamed x1, local copies, waits for them, and re-layouts  6.47 us
    another operation x1, local copies, waits for them, and re-layouts, tables(): phi = jnp.stack([jnp.where(valid, r, 0).astype(BF16) for r in rows], axis=1)  3.14 us

profile of v1, /device:TPU:0, one launch (start us, length us, event | category | flops | bytes accessed | tf_op | source)
XLA Modules:
  0.0 108.0 jit_solution(1973319375938055123)
XLA Ops:
  0.0 1.4 %reshape.1164.kind_ref = s32[1,512]{1,0:T(1,128)} reshape(s32[16,32]{1,0:T(8,128)} %param.4) | data formatting | bytes 4096 | tf_op jit(solution)/shard_map/reshape | solution.py:354
  1.4 1.3 %reshape.1165.kn_ref = f32[1,512]{1,0:T(1,128)} reshape(f32[16,32]{1,0:T(8,128)} %param.5) | data formatting | bytes 4096 | tf_op jit(solution)/shard_map/reshape | solution.py:354
  2.7 0.6 select_convert_fusion.6
  3.3 0.7 select_convert_fusion
  4.0 0.7 select_convert_fusion.4
  4.8 0.7 select_convert_fusion.2
  5.5 0.6 select_convert_fusion.16
  6.1 0.7 select_convert_fusion.14
  6.8 0.7 select_convert_fusion.12
  7.5 0.7 select_convert_fusion.10
  8.3 0.4 compare_convert_fusion
  8.7 0.4 convert_multiply_fusion
  9.1 0.4 select_convert_fusion.18
  9.6 0.7 select_convert_fusion.8
  10.3 0.2 select_convert_fusion.20
  10.5 3.1 %stack.6.phi_ref = bf16[27,32,128]{2,1,0:T(8,128)(2,1)} concatenate(bf16[27,1,128]{2,1,0:T(2,128)(2,1)S(1)} %get-tuple-element.30, bf16[27,1,128]{2,1,0:T(2,128)(2,1)S(1)} %get-tuple-element.29, bf16[27,1,128]{2,1,0:T(2,128)(2,1)S(1)} %get-tuple-element.28, bf16[27,1,128]{2,1,0:T(2,128)(2,1)S(1)} %get-tuple-element.27, bf16[27,1,128]{2,1,0:T(2,128)(2,1)S(1)} %get-tuple-element.26, ...), dimensions={1} | concatenate | bytes 442368 | tf_op jit(solution)/shard_map/stack | solution.py:39
  13.7 0.8 stack.8.lane_ref
  14.4 87.1 %shard_map.37 = f32[16,32,3456]{2,1,0:T(8,128)} custom-call(f32[16,32,3456]{2,1,0:T(8,128)} %dist.1, bf16[27,32,128]{2,1,0:T(8,128)(2,1)} %stack.6.phi_ref, f32[27,8,128]{2,1,0:T(8,128)} %stack.8.lane_ref, s32[1,512]{1,0:T(1,128)} %reshape.1164.kind_ref, f32[1,512]{1,0:T(1,128)} %reshape.1165.kn_ref), custom_call_target="tpu_custom_call" | custom-call | tf_op jit(solution)/shard_map/pallas_call | solution.py:327
  101.5 6.5 %copy.5 = f32[16,32,3456]{2,1,0:T(8,128)} copy(f32[16,32,3456]{2,1,0:T(8,128)} %shard_map.37) | data formatting | bytes 14155776
  (2 shorter events, 0.0 us)

commit v2 on v1

--- a/solution.py
+++ b/solution.py
@@ -24,31 +24,29 @@
 
 
 def tables(index, valid):
-    p = [index % NVX, index // NVX % NVX, index // (NVX * NVX)]
-    m = [(2 * (q // 2) + 1) * (2 * (q % 2) - 1) for q in p]
+    plane = jnp.floor((index + 0.5) * (1.0 / NVX))
+    c = jnp.floor((plane + 0.5) * (1.0 / NVX))
+    m = []
+    for p in (index - NVX * plane, plane - NVX * c, c):
+        pair = jnp.floor(0.5 * p)
+        m.append((2.0 * pair + 1.0) * (2.0 * (p - 2.0 * pair) - 1.0))
     x, y, z = m
     sq = x * x + y * y + z * z
     quads = [x * x, y * y, z * z, x * y, x * z, y * z]
     cubes = [x * sq, y * sq, z * sq]
-    q_hi = [(v + 8) // 16 * 16 for v in quads]
-    c_hi = [(v + 128) // 256 * 256 for v in cubes]
+    q_hi = [16.0 * jnp.floor((v + 8.0) * 0.0625) for v in quads]
+    c_hi = [256.0 * jnp.floor((v + 128.0) * 0.00390625) for v in cubes]
     q_lo = [a - b for a, b in zip(quads, q_hi)]
     c_lo = [a - b for a, b in zip(cubes, c_hi)]
     one, zero = jnp.ones_like(x), jnp.zeros_like(x)
     rows = [one, x, y, z] + q_hi + c_hi + [zero] * 3 + [zero] * 4 + q_lo + c_lo + [zero] * 3
-    phi = jnp.stack([jnp.where(valid, r, 0).astype(BF16) for r in rows], axis=1)
-    speeds = [
-        (x > 0).astype(F32),
-        (y > 0).astype(F32),
-        DT * HALF * jnp.abs(x).astype(F32),
-        DT * HALF * jnp.abs(y).astype(F32),
-    ]
-    lane = jnp.stack(speeds + [jnp.zeros_like(speeds[0])] * 4, axis=1)
-    return phi, lane
-
-
-def coefficients(s, kind, kn):
-    n = s[0]
+    phi = jnp.concatenate([jnp.where(valid, r, 0.0) for r in rows], axis=0).astype(BF16)
+    speeds = [x, y, DT * HALF * jnp.abs(x), DT * HALF * jnp.abs(y)]
+    return phi, jnp.concatenate(speeds + [zero] * 4, axis=0)
+
+
+def coefficients(s):
+    n, kind, kn = s[0], s[13], s[14]
     rho = WEIGHT * n
     u = [HALF * s[i + 1] / n for i in range(3)]
     h2 = HALF * HALF
@@ -71,7 +69,7 @@
     b = usq * inv - 5.0
     uq = u[0] * q[0] + u[1] * q[1] + u[2] * q[2]
     fk = front * kappa
-    wall, inflow = kind == 1, kind == 2
+    wall, inflow = kind == 1.0, kind == 2.0
     gas = jnp.logical_not(jnp.logical_or(wall, inflow))
     zero = jnp.zeros_like(n)
 
@@ -122,43 +120,52 @@
 
 
 def kernel(
-    sizes, group, dist, phi_ref, lane_ref, kind_ref, kn_ref, out,
-    f, g, c_send, y_send, xh, yh, acc, arg_c, poly_c, keep_c, ps,
-    in_sem, out_sem, send_sem, recv_sem, ps_send, ps_recv,
+    sizes, group, head, count, dist, kind_ref, kn_ref, out,
+    f, g, c_send, y_send, xh, yh, acc, phi_ref, lane_ref,
+    arg_c, poly_c, keep_c, arg_h, poly_h, keep_h, ps, sums, y_sums, near,
+    in_sem, out_sem, send_sem, recv_sem, ps_send, ps_recv, near_send, near_recv,
 ):
     nsx, nsy, nvel = sizes
     ncol, nx, ny = f.shape[:3]
     cells = nx * ny
+    halo = 4 * (nx + ny)
+    halo_pad = arg_h.shape[0]
     groups = ncol // group
-    x_size, y_size, v_size = nsx, nsy, nvel
     ix, iy, iv = lax.axis_index("sx"), lax.axis_index("sy"), lax.axis_index("vel")
-    x_up, x_down = lax.rem(ix + 1, x_size), lax.rem(ix + x_size - 1, x_size)
-    y_up, y_down = lax.rem(iy + 1, y_size), lax.rem(iy + y_size - 1, y_size)
+    x_up, x_down = lax.rem(ix + 1, nsx), lax.rem(ix + nsx - 1, nsx)
+    y_up, y_down = lax.rem(iy + 1, nsy), lax.rem(iy + nsy - 1, nsy)
+
+    def lanes_of(ref, j):
+        return ref.at[:, :, pl.ds(pl.multiple_of(j * LANES, LANES), LANES)]
 
     def in_copy(j):
-        return pltpu.make_async_copy(
-            dist.at[:, :, pl.ds(pl.multiple_of(j * LANES, LANES), LANES)],
-            f.at[j],
-            in_sem.at[j],
-        )
+        return pltpu.make_async_copy(lanes_of(dist, j), f.at[j], in_sem.at[j])
 
     def out_copy(j):
-        return pltpu.make_async_copy(
-            f.at[j],
-            out.at[:, :, pl.ds(pl.multiple_of(j * LANES, LANES), LANES)],
-            out_sem.at[j],
-        )
+        return pltpu.make_async_copy(f.at[j], lanes_of(out, j), out_sem.at[j])
 
     @pl.loop(0, ncol)
     def _(j):
         in_copy(j).start()
 
-    partners = [{"vel": lax.rem(iv + o, v_size)} for o in range(1, nvel)]
+    partners = [{"vel": lax.rem(iv + o, nvel)} for o in range(1, nvel)]
     partners += [{"sx": x_up}] + ([{"sx": x_down}] if nsx > 2 else [])
     partners += [{"sy": y_up}] + ([{"sy": y_down}] if nsy > 2 else [])
     barrier = pltpu.get_barrier_semaphore()
     for who in partners:
         pl.semaphore_signal(barrier, inc=1, device_id=who, device_id_type=MESH)
+
+    @pl.loop(0, ncol)
+    def _(j):
+        offset = j * LANES + lax.broadcasted_iota(jnp.int32, (1, LANES), 1)
+        phi, lane_ref[j] = tables((iv * count + offset).astype(F32), offset < count)
+        phi_ref[j] = jnp.concatenate([phi] * 4, axis=0)
+
+    kind = kind_ref[...].astype(F32)
+    kn = kn_ref[...]
+    kind_row = jnp.concatenate([kind[x : x + 1] for x in range(nx)], axis=1)
+    kn_row = jnp.concatenate([kn[x : x + 1] for x in range(nx)], axis=1)
+    acc[...] = jnp.zeros_like(acc)
     pl.semaphore_wait(barrier, len(partners))
 
     def face(slab):
@@ -175,8 +182,8 @@
             )
 
         copies = [
-            remote(0, g.at[cols, face(nx + 1)], xh.at[step, cols, 1], {"sx": x_up}),
-            remote(1, g.at[cols, face(2)], xh.at[step, cols, 2], {"sx": x_down}),
+            remote(0, f.at[cols, nx - 1], xh.at[step, cols, 1], {"sx": x_up}),
+            remote(1, f.at[cols, 0], xh.at[step, cols, 2], {"sx": x_down}),
             remote(2, c_send.at[cols], xh.at[step, cols, 0], {"sx": x_up}),
             remote(3, y_send.at[cols, 1], yh.at[step, cols, 0], {"sy": y_up}),
             remote(4, y_send.at[cols, 0], yh.at[step, cols, 1], {"sy": y_down}),
@@ -185,9 +192,32 @@
             copies.append(remote(5, c_send.at[cols], xh.at[step, cols, 3], {"sx": x_down}))
         return copies
 
+    def near_copies(step):
+        edge = 4 * ny
+
+        def remote(n, src, first, rows, who):
+            return pltpu.make_async_remote_copy(
+                src_ref=src, dst_ref=near.at[step, pl.ds(first, rows)],
+                send_sem=near_send.at[step, n], recv_sem=near_recv.at[step, n],
+                device_id=who, device_id_type=MESH,
+            )
+
+        return [
+            remote(0, sums.at[step, pl.ds(cells - 2 * ny, 2 * ny)], 0, 2 * ny, {"sx": x_up}),
+            remote(1, sums.at[step, pl.ds(0, 2 * ny)], 2 * ny, 2 * ny, {"sx": x_down}),
+            remote(2, y_sums.at[step, 1], edge, 2 * nx, {"sy": y_up}),
+            remote(3, y_sums.at[step, 0], edge + 2 * nx, 2 * nx, {"sy": y_down}),
+        ]
+
+    def pack(j):
+        pos = jnp.broadcast_to(lane_ref[j, 0:1, :], (ny, LANES)) > 0.0
+        c_send[j] = jnp.where(pos, f[j, nx - 2], f[j, 1])
+        for side, first in ((0, 0), (1, ny - 2)):
+            for layer in range(2):
+                y_send[j, side, layer * nx : (layer + 1) * nx, :] = f[j, :, first + layer, :]
+
     def add_moments(j):
-        phi = phi_ref[j]
-        wide = jnp.concatenate([phi, phi, phi, phi], axis=0)
+        wide = phi_ref[j]
         both = jnp.concatenate([wide, wide], axis=1)
         for r in range(0, cells, 128):
             val = f[j, r // ny : (r + 128) // ny].reshape(128, LANES)
@@ -206,7 +236,7 @@
             copy = pltpu.make_async_remote_copy(
                 src_ref=ps.at[step, iv], dst_ref=ps.at[step, iv],
                 send_sem=ps_send.at[step, o], recv_sem=ps_recv.at[step, o],
-                device_id={"vel": lax.rem(iv + o, v_size)}, device_id_type=MESH,
+                device_id={"vel": lax.rem(iv + o, nvel)}, device_id_type=MESH,
             )
             copy.start()
             copies.append(copy)
@@ -215,15 +245,26 @@
         total = ps[step, 0]
         for v in range(1, nvel):
             total = total + ps[step, v]
-        rows = [total[i : i + 1] for i in range(13)]
-        arg, poly, keep = coefficients(rows, kind_ref[...], kn_ref[...])
-        arg_c[...] = pieces(arg)
-        poly_c[...] = pieces(poly)
-        keep_c[...] = jnp.broadcast_to(keep, (LANES, cells)).T
+        blank = jnp.zeros((113, cells), F32)
+        total = jnp.concatenate([total[0:13], kind_row, kn_row, blank], axis=0)
+        sums[step] = total.T
+        for side, first in ((0, 0), (1, ny - 2)):
+            for layer in range(2):
+                y_sums[step, side, layer * nx : (layer + 1) * nx, :] = sums[
+                    step, pl.ds(first + layer, nx, stride=ny), :
+                ]
+        for copy in near_copies(step):
+            copy.start()
+        return total
+
+    def set_coefficients(total, arg_ref, poly_ref, keep_ref):
+        arg, poly, keep = coefficients([total[i : i + 1] for i in range(15)])
+        arg_ref[...] = pieces(arg)
+        poly_ref[...] = pieces(poly)
+        keep_ref[...] = jnp.broadcast_to(keep, (LANES, keep.shape[1])).T
 
     def relax(j):
-        phi = phi_ref[j]
-        wide = jnp.concatenate([phi, phi, phi, phi], axis=0)
+        wide = phi_ref[j]
         for r in range(0, cells, 128):
             rows = pl.ds(r, 128)
             arg = jnp.dot(arg_c[rows, :], wide, preferred_element_type=F32)
@@ -231,32 +272,31 @@
             val = f[j, r // ny : (r + 128) // ny].reshape(128, LANES)
             new = val * keep_c[rows, :] + jnp.exp(arg) * poly
             for i in range(128 // ny):
-                slab = r // ny + i + 2
-                g[j, face(slab), :] = new[i * ny : (i + 1) * ny]
-        pos = jnp.broadcast_to(lane_ref[j, 0:1, :], (ny, LANES)) > 0.0
-        c_send[j] = jnp.where(pos, g[j, face(nx), :], g[j, face(3), :])
-        for side, first in ((0, 0), (1, ny - 2)):
-            for layer in range(2):
-                y_send[j, side, layer * nx : (layer + 1) * nx, :] = g[
-                    j, pl.ds(2 * PITCH + TOP + first + layer, nx, stride=PITCH), :
-                ]
-
-    def transport(step, j):
+                g[j, face(r // ny + i + 2), :] = new[i * ny : (i + 1) * ny]
+
+    def relax_halo(step, j):
+        wide = phi_ref[j]
+        rows = pl.ds(0, halo)
+        arg = jnp.dot(arg_h[rows, :], wide, preferred_element_type=F32)
+        poly = jnp.dot(poly_h[rows, :], wide, preferred_element_type=F32)
+        far_lo = xh[step, j, 0]
+        far_hi = far_lo if nsx == 2 else xh[step, j, 3]
+        val = jnp.concatenate(
+            [far_lo, xh[step, j, 1], xh[step, j, 2], far_hi, yh[step, j, 0], yh[step, j, 1]], axis=0
+        )
+        new = val * keep_h[rows, :] + jnp.exp(arg) * poly
+        for i, slab in enumerate((0, 1, nx + 2, nx + 3)):
+            g[j, face(slab), :] = new[i * ny : (i + 1) * ny]
+        for i, first in enumerate((-2, -1, ny, ny + 1)):
+            at = 4 * ny + i * nx
+            g[j, pl.ds(2 * PITCH + TOP + first, nx, stride=PITCH), :] = new[at : at + nx]
+
+    def transport(j):
         lanes = lane_ref[j]
         pos_x = jnp.broadcast_to(lanes[0:1], (ny, LANES)) > 0.0
         pos_y = jnp.broadcast_to(lanes[1:2], (ny, LANES)) > 0.0
         rate_x = jnp.broadcast_to(lanes[2:3], (ny, LANES))
         rate_y = jnp.broadcast_to(lanes[3:4], (ny, LANES))
-        far = xh[step, j, 0]
-        g[j, face(0), :] = far
-        g[j, face(1), :] = xh[step, j, 1]
-        g[j, face(nx + 2), :] = xh[step, j, 2]
-        g[j, face(nx + 3), :] = far if nsx == 2 else xh[step, j, 3]
-        for side, first in ((0, -2), (1, ny)):
-            for layer in range(2):
-                g[j, pl.ds(2 * PITCH + TOP + first + layer, nx, stride=PITCH), :] = yh[
-                    step, j, side, layer * nx : (layer + 1) * nx, :
-                ]
         for x in range(nx):
             base = (x + 2) * PITCH + TOP
             mid = g[j, pl.ds(base, ny), :]
@@ -266,26 +306,43 @@
             div_y = upwind(pos_y, along_y[0], along_y[1], mid, along_y[2], along_y[3])
             f[j, x] = mid - (rate_x * div_x + rate_y * div_y)
 
-    acc[...] = jnp.zeros_like(acc)
-
-    @pl.loop(0, ncol)
-    def _(j):
-        in_copy(j).wait()
-        add_moments(j)
+    def send(step, k):
+        for copy in halo_copies(step, k):
+            copy.start()
+
+    @pl.loop(0, groups)
+    def _(k):
+        @pl.loop(0, group)
+        def _(i):
+            j = k * group + i
+            in_copy(j).wait()
+            pack(j)
+            add_moments(j)
+
+        @pl.when(k < head)
+        def _():
+            send(0, k)
 
     for step in range(STEPS):
         last = step == STEPS - 1
-        exchange(step)
-
-        @pl.loop(0, groups)
+        total = exchange(step)
+
+        @pl.loop(head, groups)
         def _(k):
-            @pl.loop(0, group)
-            def _(i):
-                relax(k * group + i)
-
-            for copy in halo_copies(step, k):
-                copy.start()
-
+            send(step, k)
+
+        set_coefficients(total, arg_c, poly_c, keep_c)
+
+        @pl.loop(0, ncol)
+        def _(j):
+            relax(j)
+
+        for copy in near_copies(step):
+            copy.wait()
+        around = [near[step, 0:halo, :]]
+        if halo_pad > halo:
+            around.append(sums[step, 0 : halo_pad - halo, :])
+        set_coefficients(jnp.concatenate(around, axis=0).T, arg_h, poly_h, keep_h)
         if not last:
             acc[...] = jnp.zeros_like(acc)
 
@@ -297,11 +354,18 @@
             @pl.loop(0, group)
             def _(i):
                 j = k * group + i
-                transport(step, j)
+                relax_halo(step, j)
+                transport(j)
                 if last:
                     out_copy(j).start()
                 else:
+                    pack(j)
                     add_moments(j)
+
+            if not last:
+                @pl.when(k < head)
+                def _():
+                    send(step + 1, k)
 
     @pl.loop(0, ncol)
     def _(j):
@@ -312,23 +376,22 @@
     nx, ny, count = distribution.shape
     ncol = -(-count // LANES)
     width = ncol * LANES
-    offset = jnp.arange(width, dtype=jnp.int32).reshape(ncol, LANES)
-    phi, lane = tables(lax.axis_index("vel") * count + offset, offset < count)
     padded = distribution
     if width != count:
         padded = jnp.pad(distribution, ((0, 0), (0, 0), (0, width - count)))
     group = 3 if ncol % 3 == 0 else 1
     groups, cells = ncol // group, nx * ny
+    halo_pad = -(-4 * (nx + ny) // LANES) * LANES
+    head = (4 * groups + 8) // 9
     nsx, nsy, nvel = sizes
     xcopies = 3 if nsx == 2 else 4
     dma = pltpu.SemaphoreType.DMA
-    any_spec = pl.BlockSpec(memory_space=pl.ANY)
     vmem = pl.BlockSpec(memory_space=pltpu.VMEM)
     result = pl.pallas_call(
-        functools.partial(kernel, sizes, group),
+        functools.partial(kernel, sizes, group, head, count),
         out_shape=jax.ShapeDtypeStruct((nx, ny, width), F32),
-        in_specs=[any_spec, vmem, vmem, vmem, vmem],
-        out_specs=any_spec,
+        in_specs=[pl.BlockSpec(memory_space=pltpu.MemorySpace.HBM), vmem, vmem],
+        out_specs=pl.BlockSpec(memory_space=pl.ANY),
         scratch_shapes=[
             pltpu.VMEM((ncol, nx, ny, LANES), F32),
             pltpu.VMEM((ncol, (nx + 4) * PITCH, LANES), F32),
@@ -337,21 +400,31 @@
             pltpu.VMEM((STEPS, ncol, xcopies, ny, LANES), F32),
             pltpu.VMEM((STEPS, ncol, 2, 2 * nx, LANES), F32),
             pltpu.VMEM((cells, LANES), F32),
+            pltpu.VMEM((ncol, LANES, LANES), BF16),
+            pltpu.VMEM((ncol, 8, LANES), F32),
             pltpu.VMEM((cells, LANES), BF16),
             pltpu.VMEM((cells, LANES), BF16),
             pltpu.VMEM((cells, LANES), F32),
+            pltpu.VMEM((halo_pad, LANES), BF16),
+            pltpu.VMEM((halo_pad, LANES), BF16),
+            pltpu.VMEM((halo_pad, LANES), F32),
             pltpu.VMEM((STEPS, nvel, 16, cells), F32),
+            pltpu.VMEM((STEPS, cells, LANES), F32),
+            pltpu.VMEM((STEPS, 2, 2 * nx, LANES), F32),
+            pltpu.VMEM((STEPS, 4 * (nx + ny), LANES), F32),
             dma((ncol,)),
             dma((ncol,)),
             dma((STEPS, groups, xcopies + 2)),
             dma((STEPS, groups, xcopies + 2)),
             dma((STEPS, nvel)),
             dma((STEPS, nvel)),
+            dma((STEPS, 4)),
+            dma((STEPS, 4)),
         ],
         compiler_params=pltpu.CompilerParams(
-            collective_id=0, has_side_effects=True, vmem_limit_bytes=56 * 2**20
+            collective_id=0, has_side_effects=True, vmem_limit_bytes=40 * 2**20
         ),
-    )(padded, phi, lane, cell_kind.reshape(1, cells), local_knudsen.reshape(1, cells))
+    )(padded, cell_kind, local_knudsen)
     return result[..., :count] if width != count else result
 
 

time: 108 us -> 79.7 us (0.74)
  Pallas kernels: 87.1 us -> 72 us
  other arithmetic: 7.79 us -> 0 us
  local copies, waits for them, and re-layouts: 13.1 us -> 7.36 us
    pallas_call x1, Pallas kernels: 87.1 us -> 72 us  [body(): pl.pallas_call(functools.partial(kernel, sizes, group, head, count), out_...]
    convert_element_type x12 -> x0, other arithmetic: 7.36 us -> none  [the longest x11 6.95 us: tables(): phi = jnp.stack([jnp.where(valid, r, 0).astype(BF16) for r in rows], axis=1)]
    another operation x3 -> x0, local copies, waits for them, and re-layouts: 3.91 us -> none  [the longest x1 3.14 us: tables(): phi = jnp.stack([jnp.where(valid, r, 0).astype(BF16) for r in rows], axis=1)]
    reshape x2 -> x0, local copies, waits for them, and re-layouts: 2.67 us -> none  [the longest x1 1.35 us: body(): cell_kind.reshape(1, cells)]
    unnamed x1 -> x7, local copies, waits for them, and re-layouts: 6.47 us -> 7.36 us
where the time goes in v2:
time: 79.7 us; the launch traced here: 79.4 us
  Pallas kernels  72 us (90%)
  local copies, waits for them, and re-layouts  7.36 us (9%)
    pallas_call x1, Pallas kernels, body(): pl.pallas_call(functools.partial(kernel, sizes, group, head, count), out_...  72 us
    unnamed x7, local copies, waits for them, and re-layouts  7.36 us

profile of v2, /device:TPU:0, one launch (start us, length us, event | category | flops | bytes accessed | tf_op | source)
XLA Modules:
  0.0 79.4 jit_solution(879013058814943236)
XLA Ops:
  0.0 0.0 copy-start
  0.0 3.0 %copy-done = f32[16,32,3456]{2,1,0:T(8,128)S(1)} copy-done((f32[16,32,3456]{2,1,0:T(8,128)S(1)}, f32[16,32,3456]{2,1,0:T(8,128)}, u32[]{:S(2)}) %copy-start) | copy-done | bytes 7077912
  3.0 0.0 copy-start.1
  3.0 0.7 copy-done.1
  3.7 0.0 copy-start.2
  3.7 0.7 copy-done.2
  4.4 72.0 %shard_map.37 = f32[16,32,3456]{2,1,0:T(8,128)S(1)} custom-call(f32[16,32,3456]{2,1,0:T(8,128)S(1)} %copy-done, s32[16,32]{1,0:T(8,128)S(1)} %copy-done.1, f32[16,32]{1,0:T(8,128)S(1)} %copy-done.2), custom_call_target="tpu_custom_call" | custom-call | tf_op jit(solution)/shard_map/pallas_call | solution.py:390
  76.4 3.0 %copy.5 = f32[16,32,3456]{2,1,0:T(8,128)} copy(f32[16,32,3456]{2,1,0:T(8,128)S(1)} %shard_map.37) | data formatting | bytes 14155776
Async XLA Ops:
  0.0 3.0 %copy-start = (f32[16,32,3456]{2,1,0:T(8,128)S(1)}, f32[16,32,3456]{2,1,0:T(8,128)}, u32[]{:S(2)}) copy-start(f32[16,32,3456]{2,1,0:T(8,128)} %dist.1) | copy-start | bytes 21233668
  3.0 0.7 copy-start.1
  3.7 0.7 copy-start.2

commit v3 on v2

--- a/solution.py
+++ b/solution.py
@@ -41,7 +41,7 @@
     one, zero = jnp.ones_like(x), jnp.zeros_like(x)
     rows = [one, x, y, z] + q_hi + c_hi + [zero] * 3 + [zero] * 4 + q_lo + c_lo + [zero] * 3
     phi = jnp.concatenate([jnp.where(valid, r, 0.0) for r in rows], axis=0).astype(BF16)
-    speeds = [x, y, DT * HALF * jnp.abs(x), DT * HALF * jnp.abs(y)]
+    speeds = [x, y, DT * HALF * x, DT * HALF * jnp.abs(y)]
     return phi, jnp.concatenate(speeds + [zero] * 4, axis=0)
 
 
@@ -120,10 +120,10 @@
 
 
 def kernel(
-    sizes, group, head, count, dist, kind_ref, kn_ref, out,
-    f, g, c_send, y_send, xh, yh, acc, phi_ref, lane_ref,
+    sizes, group, head, count, dist, kind_in, kn_in, out,
+    kind_ref, kn_ref, f, g, c_send, y_send, xh, yh, acc, phi_ref, lane_ref,
     arg_c, poly_c, keep_c, arg_h, poly_h, keep_h, ps, sums, y_sums, near,
-    in_sem, out_sem, send_sem, recv_sem, ps_send, ps_recv, near_send, near_recv,
+    cell_sem, in_sem, out_sem, send_sem, recv_sem, ps_send, ps_recv, near_send, near_recv,
 ):
     nsx, nsy, nvel = sizes
     ncol, nx, ny = f.shape[:3]
@@ -144,9 +144,17 @@
     def out_copy(j):
         return pltpu.make_async_copy(f.at[j], lanes_of(out, j), out_sem.at[j])
 
+    cell_copies = [
+        pltpu.make_async_copy(kind_in, kind_ref, cell_sem.at[0]),
+        pltpu.make_async_copy(kn_in, kn_ref, cell_sem.at[1]),
+    ]
+
     @pl.loop(0, ncol)
     def _(j):
         in_copy(j).start()
+
+    for copy in cell_copies:
+        copy.start()
 
     partners = [{"vel": lax.rem(iv + o, nvel)} for o in range(1, nvel)]
     partners += [{"sx": x_up}] + ([{"sx": x_down}] if nsx > 2 else [])
@@ -155,16 +163,6 @@
     for who in partners:
         pl.semaphore_signal(barrier, inc=1, device_id=who, device_id_type=MESH)
 
-    @pl.loop(0, ncol)
-    def _(j):
-        offset = j * LANES + lax.broadcasted_iota(jnp.int32, (1, LANES), 1)
-        phi, lane_ref[j] = tables((iv * count + offset).astype(F32), offset < count)
-        phi_ref[j] = jnp.concatenate([phi] * 4, axis=0)
-
-    kind = kind_ref[...].astype(F32)
-    kn = kn_ref[...]
-    kind_row = jnp.concatenate([kind[x : x + 1] for x in range(nx)], axis=1)
-    kn_row = jnp.concatenate([kn[x : x + 1] for x in range(nx)], axis=1)
     acc[...] = jnp.zeros_like(acc)
     pl.semaphore_wait(barrier, len(partners))
 
@@ -208,6 +206,11 @@
             remote(2, y_sums.at[step, 1], edge, 2 * nx, {"sy": y_up}),
             remote(3, y_sums.at[step, 0], edge + 2 * nx, 2 * nx, {"sy": y_down}),
         ]
+
+    def build_tables(j):
+        offset = j * LANES + lax.broadcasted_iota(jnp.int32, (1, LANES), 1)
+        phi, lane_ref[j] = tables((iv * count + offset).astype(F32), offset < count)
+        phi_ref[j] = jnp.concatenate([phi] * 4, axis=0)
 
     def pack(j):
         pos = jnp.broadcast_to(lane_ref[j, 0:1, :], (ny, LANES)) > 0.0
@@ -292,19 +295,37 @@
             g[j, pl.ds(2 * PITCH + TOP + first, nx, stride=PITCH), :] = new[at : at + nx]
 
     def transport(j):
-        lanes = lane_ref[j]
-        pos_x = jnp.broadcast_to(lanes[0:1], (ny, LANES)) > 0.0
-        pos_y = jnp.broadcast_to(lanes[1:2], (ny, LANES)) > 0.0
-        rate_x = jnp.broadcast_to(lanes[2:3], (ny, LANES))
-        rate_y = jnp.broadcast_to(lanes[3:4], (ny, LANES))
-        for x in range(nx):
-            base = (x + 2) * PITCH + TOP
-            mid = g[j, pl.ds(base, ny), :]
-            along_x = [g[j, pl.ds(base + d * PITCH, ny), :] for d in (-2, -1, 1, 2)]
-            along_y = [g[j, pl.ds(base + d, ny), :] for d in (-2, -1, 1, 2)]
-            div_x = upwind(pos_x, along_x[0], along_x[1], mid, along_x[2], along_x[3])
-            div_y = upwind(pos_y, along_y[0], along_y[1], mid, along_y[2], along_y[3])
-            f[j, x] = mid - (rate_x * div_x + rate_y * div_y)
+        half = ny // 2
+        lanes = [jnp.broadcast_to(lane_ref[j, i : i + 1, :], (half, LANES)) for i in range(4)]
+        pos_x, pos_y = lanes[0] > 0.0, lanes[1] > 0.0
+        side_x = jnp.where(pos_x, 0.5, -0.5)
+        rate_x, rate_y = lanes[2:]
+        for row in (0, half):
+
+            def cells_at(x, d=0):
+                return g[j, pl.ds((x + 2) * PITCH + TOP + row + d, half), :]
+
+            low, mid = cells_at(-2), cells_at(-1)
+            diff = mid - low
+            kept = face_value = flux = None
+            for x in range(-1, nx + 1):
+                high = cells_at(x + 1)
+                ahead = high - mid
+                slope = jnp.minimum(
+                    jnp.maximum(ahead, jnp.minimum(diff, 0.0)), jnp.maximum(diff, 0.0)
+                )
+                value = mid + side_x * slope
+                if x >= 0:
+                    new_flux = jnp.where(pos_x, face_value, value)
+                if x >= 1:
+                    along = [cells_at(x - 1, d) for d in (-2, -1, 1, 2)]
+                    div_y = upwind(pos_y, along[0], along[1], kept, along[2], along[3])
+                    f[j, x - 1, row : row + half, :] = kept - (
+                        rate_x * (new_flux - flux) + rate_y * div_y
+                    )
+                if x >= 0:
+                    flux = new_flux
+                kept, face_value, mid, diff = mid, value, high, ahead
 
     def send(step, k):
         for copy in halo_copies(step, k):
@@ -315,13 +336,24 @@
         @pl.loop(0, group)
         def _(i):
             j = k * group + i
+            build_tables(j)
             in_copy(j).wait()
             pack(j)
-            add_moments(j)
 
         @pl.when(k < head)
         def _():
             send(0, k)
+
+        @pl.loop(0, group)
+        def _(i):
+            add_moments(k * group + i)
+
+    for copy in cell_copies:
+        copy.wait()
+    kind = kind_ref[...].astype(F32)
+    kn = kn_ref[...]
+    kind_row = jnp.concatenate([kind[x : x + 1] for x in range(nx)], axis=1)
+    kn_row = jnp.concatenate([kn[x : x + 1] for x in range(nx)], axis=1)
 
     for step in range(STEPS):
         last = step == STEPS - 1
@@ -360,12 +392,15 @@
                     out_copy(j).start()
                 else:
                     pack(j)
-                    add_moments(j)
 
             if not last:
                 @pl.when(k < head)
                 def _():
                     send(step + 1, k)
+
+                @pl.loop(0, group)
+                def _(i):
+                    add_moments(k * group + i)
 
     @pl.loop(0, ncol)
     def _(j):
@@ -386,13 +421,18 @@
     nsx, nsy, nvel = sizes
     xcopies = 3 if nsx == 2 else 4
     dma = pltpu.SemaphoreType.DMA
-    vmem = pl.BlockSpec(memory_space=pltpu.VMEM)
+    operands = [
+        pltpu.with_memory_space_constraint(a, pltpu.MemorySpace.HBM)
+        for a in (padded, cell_kind, local_knudsen)
+    ]
     result = pl.pallas_call(
         functools.partial(kernel, sizes, group, head, count),
         out_shape=jax.ShapeDtypeStruct((nx, ny, width), F32),
-        in_specs=[pl.BlockSpec(memory_space=pltpu.MemorySpace.HBM), vmem, vmem],
+        in_specs=[pl.BlockSpec(memory_space=pltpu.MemorySpace.HBM)] * 3,
         out_specs=pl.BlockSpec(memory_space=pl.ANY),
         scratch_shapes=[
+            pltpu.VMEM((nx, ny), jnp.int32),
+            pltpu.VMEM((nx, ny), F32),
             pltpu.VMEM((ncol, nx, ny, LANES), F32),
             pltpu.VMEM((ncol, (nx + 4) * PITCH, LANES), F32),
             pltpu.VMEM((ncol, ny, LANES), F32),
@@ -412,6 +452,7 @@
             pltpu.VMEM((STEPS, cells, LANES), F32),
             pltpu.VMEM((STEPS, 2, 2 * nx, LANES), F32),
             pltpu.VMEM((STEPS, 4 * (nx + ny), LANES), F32),
+            dma((2,)),
             dma((ncol,)),
             dma((ncol,)),
             dma((STEPS, groups, xcopies + 2)),
@@ -424,7 +465,7 @@
         compiler_params=pltpu.CompilerParams(
             collective_id=0, has_side_effects=True, vmem_limit_bytes=40 * 2**20
         ),
-    )(padded, cell_kind, local_knudsen)
+    )(*operands)
     return result[..., :count] if width != count else result
 
 

time: 79.7 us -> 74.1 us (0.930)
  local copies, waits for them, and re-layouts: 7.36 us -> 2.96 us
  Pallas kernels: 72 us -> 70.9 us
    unnamed x7 -> x1, local copies, waits for them, and re-layouts: 7.36 us -> 2.96 us
    pallas_call x1, Pallas kernels: 72 us -> 70.9 us  [body(): pl.pallas_call(functools.partial(kernel, sizes, group, head, count), out_...]
where the time goes in v3:
time: 74.1 us; the launch traced here: 73.9 us
  Pallas kernels  70.9 us (96%)
  local copies, waits for them, and re-layouts  2.96 us (4%)
    pallas_call x1, Pallas kernels, body(): pl.pallas_call(functools.partial(kernel, sizes, group, head, count), out_...  70.9 us
    unnamed x1, local copies, waits for them, and re-layouts  2.96 us

profile of v3, /device:TPU:0, one launch (start us, length us, event | category | flops | bytes accessed | tf_op | source)
XLA Modules:
  0.0 73.9 jit_solution(1552122786245204391)
XLA Ops:
  0.0 70.9 %shard_map.37 = f32[16,32,3456]{2,1,0:T(8,128)S(1)} custom-call(f32[16,32,3456]{2,1,0:T(8,128)} %dist.1, s32[16,32]{1,0:T(8,128)} %kind_in.1, f32[16,32]{1,0:T(8,128)} %kn_in.1), custom_call_target="tpu_custom_call" | custom-call | tf_op jit(solution)/shard_map/pallas_call | solution.py:428
  71.0 3.0 %copy.5 = f32[16,32,3456]{2,1,0:T(8,128)} copy(f32[16,32,3456]{2,1,0:T(8,128)S(1)} %shard_map.37) | data formatting | bytes 14155776

commit v4 on v3

--- a/solution.py
+++ b/solution.py
@@ -120,7 +120,7 @@
 
 
 def kernel(
-    sizes, group, head, count, dist, kind_in, kn_in, out,
+    sizes, count, dist, kind_in, kn_in, out,
     kind_ref, kn_ref, f, g, c_send, y_send, xh, yh, acc, phi_ref, lane_ref,
     arg_c, poly_c, keep_c, arg_h, poly_h, keep_h, ps, sums, y_sums, near,
     cell_sem, in_sem, out_sem, send_sem, recv_sem, ps_send, ps_recv, near_send, near_recv,
@@ -130,7 +130,10 @@
     cells = nx * ny
     halo = 4 * (nx + ny)
     halo_pad = arg_h.shape[0]
-    groups = ncol // group
+    first = 2 * ((2 * ncol + 4) // 9)
+    more = first + 2 * ncol // 9
+    window = more - ncol // 3
+    late = ncol - first // 2
     ix, iy, iv = lax.axis_index("sx"), lax.axis_index("sy"), lax.axis_index("vel")
     x_up, x_down = lax.rem(ix + 1, nsx), lax.rem(ix + nsx - 1, nsx)
     y_up, y_down = lax.rem(iy + 1, nsy), lax.rem(iy + nsy - 1, nsy)
@@ -169,13 +172,12 @@
     def face(slab):
         return pl.ds(slab * PITCH + TOP, ny)
 
-    def halo_copies(step, k):
-        cols = pl.ds(k * group, group)
+    def halo_copies(step, cols):
 
         def remote(n, src, dst, who):
             return pltpu.make_async_remote_copy(
                 src_ref=src, dst_ref=dst,
-                send_sem=send_sem.at[step, k, n], recv_sem=recv_sem.at[step, k, n],
+                send_sem=send_sem.at[step, cols, n], recv_sem=recv_sem.at[step, cols, n],
                 device_id=who, device_id_type=MESH,
             )
 
@@ -215,9 +217,9 @@
     def pack(j):
         pos = jnp.broadcast_to(lane_ref[j, 0:1, :], (ny, LANES)) > 0.0
         c_send[j] = jnp.where(pos, f[j, nx - 2], f[j, 1])
-        for side, first in ((0, 0), (1, ny - 2)):
+        for side, row in ((0, 0), (1, ny - 2)):
             for layer in range(2):
-                y_send[j, side, layer * nx : (layer + 1) * nx, :] = f[j, :, first + layer, :]
+                y_send[j, side, layer * nx : (layer + 1) * nx, :] = f[j, :, row + layer, :]
 
     def add_moments(j):
         wide = phi_ref[j]
@@ -251,10 +253,10 @@
         blank = jnp.zeros((113, cells), F32)
         total = jnp.concatenate([total[0:13], kind_row, kn_row, blank], axis=0)
         sums[step] = total.T
-        for side, first in ((0, 0), (1, ny - 2)):
+        for side, row in ((0, 0), (1, ny - 2)):
             for layer in range(2):
                 y_sums[step, side, layer * nx : (layer + 1) * nx, :] = sums[
-                    step, pl.ds(first + layer, nx, stride=ny), :
+                    step, pl.ds(row + layer, nx, stride=ny), :
                 ]
         for copy in near_copies(step):
             copy.start()
@@ -331,22 +333,17 @@
         for copy in halo_copies(step, k):
             copy.start()
 
-    @pl.loop(0, groups)
-    def _(k):
-        @pl.loop(0, group)
-        def _(i):
-            j = k * group + i
-            build_tables(j)
-            in_copy(j).wait()
-            pack(j)
-
-        @pl.when(k < head)
+    @pl.loop(0, ncol)
+    def _(j):
+        build_tables(j)
+        in_copy(j).wait()
+        pack(j)
+
+        @pl.when(j < first)
         def _():
-            send(0, k)
-
-        @pl.loop(0, group)
-        def _(i):
-            add_moments(k * group + i)
+            send(0, j)
+
+        add_moments(j)
 
     for copy in cell_copies:
         copy.wait()
@@ -359,9 +356,9 @@
         last = step == STEPS - 1
         total = exchange(step)
 
-        @pl.loop(head, groups)
-        def _(k):
-            send(step, k)
+        @pl.loop(first, more)
+        def _(j):
+            send(step, j)
 
         set_coefficients(total, arg_c, poly_c, keep_c)
 
@@ -378,29 +375,28 @@
         if not last:
             acc[...] = jnp.zeros_like(acc)
 
-        @pl.loop(0, groups)
-        def _(k):
-            for copy in halo_copies(step, k):
+        @pl.loop(0, ncol)
+        def _(j):
+            for copy in halo_copies(step, j):
                 copy.wait()
 
-            @pl.loop(0, group)
-            def _(i):
-                j = k * group + i
-                relax_halo(step, j)
-                transport(j)
-                if last:
-                    out_copy(j).start()
-                else:
-                    pack(j)
-
-            if not last:
-                @pl.when(k < head)
+            @pl.when((j >= more - window) & (j < ncol - window))
+            def _():
+                send(step, j + window)
+
+            relax_halo(step, j)
+            transport(j)
+            if last:
+                out_copy(j).start()
+            else:
+                pack(j)
+
+                @pl.when(j >= late)
                 def _():
-                    send(step + 1, k)
-
-                @pl.loop(0, group)
-                def _(i):
-                    add_moments(k * group + i)
+                    send(step + 1, 2 * (j - late))
+                    send(step + 1, 2 * (j - late) + 1)
+
+                add_moments(j)
 
     @pl.loop(0, ncol)
     def _(j):
@@ -414,10 +410,8 @@
     padded = distribution
     if width != count:
         padded = jnp.pad(distribution, ((0, 0), (0, 0), (0, width - count)))
-    group = 3 if ncol % 3 == 0 else 1
-    groups, cells = ncol // group, nx * ny
+    cells = nx * ny
     halo_pad = -(-4 * (nx + ny) // LANES) * LANES
-    head = (4 * groups + 8) // 9
     nsx, nsy, nvel = sizes
     xcopies = 3 if nsx == 2 else 4
     dma = pltpu.SemaphoreType.DMA
@@ -426,7 +420,7 @@
         for a in (padded, cell_kind, local_knudsen)
     ]
     result = pl.pallas_call(
-        functools.partial(kernel, sizes, group, head, count),
+        functools.partial(kernel, sizes, count),
         out_shape=jax.ShapeDtypeStruct((nx, ny, width), F32),
         in_specs=[pl.BlockSpec(memory_space=pltpu.MemorySpace.HBM)] * 3,
         out_specs=pl.BlockSpec(memory_space=pl.ANY),
@@ -455,8 +449,8 @@
             dma((2,)),
             dma((ncol,)),
             dma((ncol,)),
-            dma((STEPS, groups, xcopies + 2)),
-            dma((STEPS, groups, xcopies + 2)),
+            dma((STEPS, ncol, xcopies + 2)),
+            dma((STEPS, ncol, xcopies + 2)),
             dma((STEPS, nvel)),
             dma((STEPS, nvel)),
             dma((STEPS, 4)),

time: 74.1 us -> 82.4 us (1.11)
  Pallas kernels: 70.9 us -> 79.3 us
    pallas_call x1, Pallas kernels: 70.9 us -> 79.3 us  [body(): pl.pallas_call(functools.partial(kernel, sizes, count), out_shape=jax.Sha...]
where the time goes in v4:
time: 82.4 us; the launch traced here: 82.3 us
  Pallas kernels  79.3 us (96%)
  local copies, waits for them, and re-layouts  2.96 us (4%)
    pallas_call x1, Pallas kernels, body(): pl.pallas_call(functools.partial(kernel, sizes, count), out_shape=jax.Sha...  79.3 us
    unnamed x1, local copies, waits for them, and re-layouts  2.96 us

profile of v4, /device:TPU:0, one launch (start us, length us, event | category | flops | bytes accessed | tf_op | source)
XLA Modules:
  0.0 82.3 jit_solution(10340147471214617763)
XLA Ops:
  0.0 79.3 %shard_map.37 = f32[16,32,3456]{2,1,0:T(8,128)S(1)} custom-call(f32[16,32,3456]{2,1,0:T(8,128)} %dist.1, s32[16,32]{1,0:T(8,128)} %kind_in.1, f32[16,32]{1,0:T(8,128)} %kn_in.1), custom_call_target="tpu_custom_call" | custom-call | tf_op jit(solution)/shard_map/pallas_call | solution.py:422
  79.3 3.0 %copy.5 = f32[16,32,3456]{2,1,0:T(8,128)} copy(f32[16,32,3456]{2,1,0:T(8,128)S(1)} %shard_map.37) | data formatting | bytes 14155776

commit v5 on v3

--- a/solution.py
+++ b/solution.py
@@ -121,7 +121,7 @@
 
 def kernel(
     sizes, group, head, count, dist, kind_in, kn_in, out,
-    kind_ref, kn_ref, f, g, c_send, y_send, xh, yh, acc, phi_ref, lane_ref,
+    kind_ref, kn_ref, f, g, x_send, y_send, xh, yh, acc, phi_ref, lane_ref,
     arg_c, poly_c, keep_c, arg_h, poly_h, keep_h, ps, sums, y_sums, near,
     cell_sem, in_sem, out_sem, send_sem, recv_sem, ps_send, ps_recv, near_send, near_recv,
 ):
@@ -164,7 +164,6 @@
         pl.semaphore_signal(barrier, inc=1, device_id=who, device_id_type=MESH)
 
     acc[...] = jnp.zeros_like(acc)
-    pl.semaphore_wait(barrier, len(partners))
 
     def face(slab):
         return pl.ds(slab * PITCH + TOP, ny)
@@ -180,14 +179,17 @@
             )
 
         copies = [
-            remote(0, f.at[cols, nx - 1], xh.at[step, cols, 1], {"sx": x_up}),
-            remote(1, f.at[cols, 0], xh.at[step, cols, 2], {"sx": x_down}),
-            remote(2, c_send.at[cols], xh.at[step, cols, 0], {"sx": x_up}),
-            remote(3, y_send.at[cols, 1], yh.at[step, cols, 0], {"sy": y_up}),
-            remote(4, y_send.at[cols, 0], yh.at[step, cols, 1], {"sy": y_down}),
+            remote(0, y_send.at[cols, 1], yh.at[step, cols, 0], {"sy": y_up}),
+            remote(1, y_send.at[cols, 0], yh.at[step, cols, 1], {"sy": y_down}),
         ]
-        if nsx > 2:
-            copies.append(remote(5, c_send.at[cols], xh.at[step, cols, 3], {"sx": x_down}))
+        if nsx == 2:
+            return [remote(2, x_send.at[cols], xh.at[step, cols], {"sx": x_up})] + copies
+        copies += [
+            remote(2, x_send.at[cols, 0], xh.at[step, cols, 0], {"sx": x_up}),
+            remote(3, x_send.at[cols, 1], xh.at[step, cols, 1], {"sx": x_up}),
+            remote(4, x_send.at[cols, 2], xh.at[step, cols, 2], {"sx": x_down}),
+            remote(5, x_send.at[cols, 0], xh.at[step, cols, 3], {"sx": x_down}),
+        ]
         return copies
 
     def near_copies(step):
@@ -214,7 +216,9 @@
 
     def pack(j):
         pos = jnp.broadcast_to(lane_ref[j, 0:1, :], (ny, LANES)) > 0.0
-        c_send[j] = jnp.where(pos, f[j, nx - 2], f[j, 1])
+        x_send[j, 0] = jnp.where(pos, f[j, nx - 2], f[j, 1])
+        x_send[j, 1] = f[j, nx - 1]
+        x_send[j, 2] = f[j, 0]
         for side, first in ((0, 0), (1, ny - 2)):
             for layer in range(2):
                 y_send[j, side, layer * nx : (layer + 1) * nx, :] = f[j, :, first + layer, :]
@@ -331,14 +335,22 @@
         for copy in halo_copies(step, k):
             copy.start()
 
-    @pl.loop(0, groups)
-    def _(k):
+    def prepare(k):
         @pl.loop(0, group)
         def _(i):
             j = k * group + i
             build_tables(j)
             in_copy(j).wait()
             pack(j)
+
+    prepare(0)
+    pl.semaphore_wait(barrier, len(partners))
+
+    @pl.loop(0, groups)
+    def _(k):
+        @pl.when(k > 0)
+        def _():
+            prepare(k)
 
         @pl.when(k < head)
         def _():
@@ -435,7 +447,7 @@
             pltpu.VMEM((nx, ny), F32),
             pltpu.VMEM((ncol, nx, ny, LANES), F32),
             pltpu.VMEM((ncol, (nx + 4) * PITCH, LANES), F32),
-            pltpu.VMEM((ncol, ny, LANES), F32),
+            pltpu.VMEM((ncol, 3, ny, LANES), F32),
             pltpu.VMEM((ncol, 2, 2 * nx, LANES), F32),
             pltpu.VMEM((STEPS, ncol, xcopies, ny, LANES), F32),
             pltpu.VMEM((STEPS, ncol, 2, 2 * nx, LANES), F32),
@@ -455,8 +467,8 @@
             dma((2,)),
             dma((ncol,)),
             dma((ncol,)),
-            dma((STEPS, groups, xcopies + 2)),
-            dma((STEPS, groups, xcopies + 2)),
+            dma((STEPS, groups, 3 if nsx == 2 else 6)),
+            dma((STEPS, groups, 3 if nsx == 2 else 6)),
             dma((STEPS, nvel)),
             dma((STEPS, nvel)),
             dma((STEPS, 4)),

time: 74.1 us -> 73.1 us (0.987)
  Pallas kernels: 70.9 us -> 69.9 us
    pallas_call x1, Pallas kernels: 70.9 us -> 69.9 us  [body(): pl.pallas_call(functools.partial(kernel, sizes, group, head, count), out_...]
where the time goes in v5:
time: 73.1 us; the launch traced here: 72.9 us
  Pallas kernels  69.9 us (96%)
  local copies, waits for them, and re-layouts  2.96 us (4%)
    pallas_call x1, Pallas kernels, body(): pl.pallas_call(functools.partial(kernel, sizes, group, head, count), out_...  69.9 us
    unnamed x1, local copies, waits for them, and re-layouts  2.96 us

profile of v5, /device:TPU:0, one launch (start us, length us, event | category | flops | bytes accessed | tf_op | source)
XLA Modules:
  0.0 72.9 jit_solution(7908677319974763417)
XLA Ops:
  0.0 69.9 %shard_map.37 = f32[16,32,3456]{2,1,0:T(8,128)S(1)} custom-call(f32[16,32,3456]{2,1,0:T(8,128)} %dist.1, s32[16,32]{1,0:T(8,128)} %kind_in.1, f32[16,32]{1,0:T(8,128)} %kn_in.1), custom_call_target="tpu_custom_call" | custom-call | tf_op jit(solution)/shard_map/pallas_call | solution.py:440
  70.0 3.0 %copy.5 = f32[16,32,3456]{2,1,0:T(8,128)} copy(f32[16,32,3456]{2,1,0:T(8,128)S(1)} %shard_map.37) | data formatting | bytes 14155776

commit v6 on v5

--- a/solution.py
+++ b/solution.py
@@ -168,13 +168,14 @@
     def face(slab):
         return pl.ds(slab * PITCH + TOP, ny)
 
-    def halo_copies(step, k):
-        cols = pl.ds(k * group, group)
+    def halo_copies(step, k, tail=None):
+        cols = pl.ds(k * group, group) if tail is None else pl.ds(k * group + tail, 1)
+        slot = k if tail is None else k + tail
 
         def remote(n, src, dst, who):
             return pltpu.make_async_remote_copy(
                 src_ref=src, dst_ref=dst,
-                send_sem=send_sem.at[step, k, n], recv_sem=recv_sem.at[step, k, n],
+                send_sem=send_sem.at[step, slot, n], recv_sem=recv_sem.at[step, slot, n],
                 device_id=who, device_id_type=MESH,
             )
 
@@ -371,9 +372,13 @@
         last = step == STEPS - 1
         total = exchange(step)
 
-        @pl.loop(head, groups)
+        @pl.loop(head, groups - 1)
         def _(k):
             send(step, k)
+
+        for i in range(group):
+            for copy in halo_copies(step, groups - 1, i):
+                copy.start()
 
         set_coefficients(total, arg_c, poly_c, keep_c)
 
@@ -390,7 +395,7 @@
         if not last:
             acc[...] = jnp.zeros_like(acc)
 
-        @pl.loop(0, groups)
+        @pl.loop(0, groups - 1)
         def _(k):
             for copy in halo_copies(step, k):
                 copy.wait()
@@ -413,6 +418,19 @@
                 @pl.loop(0, group)
                 def _(i):
                     add_moments(k * group + i)
+
+        @pl.loop(0, group)
+        def _(i):
+            for copy in halo_copies(step, groups - 1, i):
+                copy.wait()
+            j = (groups - 1) * group + i
+            relax_halo(step, j)
+            transport(j)
+            if last:
+                out_copy(j).start()
+            else:
+                pack(j)
+                add_moments(j)
 
     @pl.loop(0, ncol)
     def _(j):
@@ -429,7 +447,7 @@
     group = 3 if ncol % 3 == 0 else 1
     groups, cells = ncol // group, nx * ny
     halo_pad = -(-4 * (nx + ny) // LANES) * LANES
-    head = (4 * groups + 8) // 9
+    head = min((4 * groups + 8) // 9, groups - 1)
     nsx, nsy, nvel = sizes
     xcopies = 3 if nsx == 2 else 4
     dma = pltpu.SemaphoreType.DMA
@@ -467,8 +485,8 @@
             dma((2,)),
             dma((ncol,)),
             dma((ncol,)),
-            dma((STEPS, groups, 3 if nsx == 2 else 6)),
-            dma((STEPS, groups, 3 if nsx == 2 else 6)),
+            dma((STEPS, groups + group - 1, 3 if nsx == 2 else 6)),
+            dma((STEPS, groups + group - 1, 3 if nsx == 2 else 6)),
             dma((STEPS, nvel)),
             dma((STEPS, nvel)),
             dma((STEPS, 4)),

time: 73.1 us -> 72.5 us (level)
  no operation moved by 1% of the time
where the time goes in v6:
time: 72.5 us; the launch traced here: 72.4 us
  Pallas kernels  69.4 us (96%)
  local copies, waits for them, and re-layouts  2.96 us (4%)
    pallas_call x1, Pallas kernels, body(): pl.pallas_call(functools.partial(kernel, sizes, group, head, count), out_...  69.4 us
    unnamed x1, local copies, waits for them, and re-layouts  2.96 us

profile of v6, /device:TPU:0, one launch (start us, length us, event | category | flops | bytes accessed | tf_op | source)
XLA Modules:
  0.0 72.4 jit_solution(7181571415724963365)
XLA Ops:
  0.0 69.4 %shard_map.37 = f32[16,32,3456]{2,1,0:T(8,128)S(1)} custom-call(f32[16,32,3456]{2,1,0:T(8,128)} %dist.1, s32[16,32]{1,0:T(8,128)} %kind_in.1, f32[16,32]{1,0:T(8,128)} %kn_in.1), custom_call_target="tpu_custom_call" | custom-call | tf_op jit(solution)/shard_map/pallas_call | solution.py:458
  69.4 3.0 %copy.5 = f32[16,32,3456]{2,1,0:T(8,128)} copy(f32[16,32,3456]{2,1,0:T(8,128)S(1)} %shard_map.37) | data formatting | bytes 14155776
